TPU v7x, 512 devices: a whole 4x8x8 slice. The times are simulated.
512 devices in a mesh: modes: 4 (over y_lo), elems: 128 (over z, y_hi, x, core).
Axes of the slice: x: 4, y: 8 (y_hi: 2, y_lo: 4; y = y_hi * 4 + y_lo), z: 8, core: 2. Of those that a mesh axis runs over, the one named last changes fastest.
Arguments:
- state: float32 [512, 3, 2, 64, 512], P('elems', None, None, None, 'modes'), may hold values from -3 to 3
- adjoint_end: float32 [512, 3, 2, 64, 512], P('elems', None, None, None, 'modes'), may hold values from -6 to 6
- observed: bfloat16 [512, 3, 2, 64, 512], P('elems', None, None, None, 'modes'), may hold values from -3 to 3
- spacing: float32 [512, 2], P('elems'), may hold values from 0.5 to 2
- radial_slot: int32 [128, 4], P('elems'), may hold values from 0 to 3, each once within a row
Outputs:
- next_state: float32 [512, 3, 2, 64, 512], P('elems', None, None, None, 'modes')
- adjoint_start: float32 [512, 3, 2, 64, 512], P('elems', None, None, None, 'modes')
Inputs may be any that keep to these rules, and one draw needn't show every extreme that they name: `radial_slot`: each row lists every radial row 0 to 3 once.
All inputs are finite; a program needn't handle non-finite values.
Results may differ from a plain program's by a relative error of at most 0.017.
Values may be sent and summed in bfloat16 or wider, within the bound.
A program may use at most 64 MiB of HBM per device.

v0:
```python
import jax
import jax.numpy as jnp
import numpy as np
from jax import lax
from jax.sharding import PartitionSpec as P

GLL = 8


time_step = 0.01
viscosity = 0.05
wave_scale = 4.0
exact_precision = lax.Precision.HIGHEST
pair_order = ((0, 0), (0, 1), (0, 2), (1, 1), (1, 2), (2, 2))
pair_index = ((0, 1, 2), (1, 3, 4), (2, 4, 5))


def with_halo(block, sides, width):
    for axis, dim in sides:
        count = lax.axis_size(axis)
        forward = [(i, i + 1) for i in range(count - 1)]
        forward.append((count - 1, 0))
        backward = [(target, source) for source, target in forward]
        low = lax.ppermute(
            lax.slice_in_dim(block, block.shape[dim] - width, None, axis=dim), axis, forward
        )
        high = lax.ppermute(lax.slice_in_dim(block, 0, width, axis=dim), axis, backward)
        block = jnp.concatenate([low, block, high], axis=dim)
    return block


def legendre_table(points, quad_count):
    columns = [points * 0.0 + 1.0, points]
    for degree in range(2, quad_count):
        columns.append(
            ((2 * degree - 1) * points * columns[-1] - (degree - 1) * columns[-2]) / degree
        )
    return np.stack(columns, axis=1)


def gll_tables(quad_count):
    degree = quad_count - 1
    points = -np.cos(np.pi * np.arange(quad_count) / degree)
    for repeat in range(60):
        vander = legendre_table(points, quad_count)
        points = points - (points * vander[:, degree] - vander[:, degree - 1]) / (
            quad_count * vander[:, degree]
        )
    vander = legendre_table(points, quad_count)
    edge_value = vander[:, degree]
    weights = 2.0 / (degree * quad_count * edge_value * edge_value)
    diagonal_mask = np.arange(quad_count)[:, None] == np.arange(quad_count)[None, :]
    differ = np.where(diagonal_mask, 1.0, points[:, None] - points[None, :])
    derivative = np.where(diagonal_mask, 0.0, edge_value[:, None] / (edge_value[None, :] * differ))
    derivative[0, 0] = -degree * quad_count / 4.0
    derivative[degree, degree] = degree * quad_count / 4.0
    return (weights, derivative)


def fourier_tables(mode_total, plane_total):
    product = np.outer(np.arange(mode_total), np.arange(plane_total)) % plane_total
    angles = 2.0 * np.pi * product / plane_total
    factor = np.where(np.arange(mode_total) == 0, 1.0, 2.0)[:, None]
    synthesis = np.stack((factor * np.cos(angles), -factor * np.sin(angles)))
    analysis_field = np.stack((np.cos(angles), -np.sin(angles))) / plane_total
    return (synthesis, np.transpose(analysis_field, (2, 0, 1)))


def quad_weights(spacing, weights):
    area = spacing[:, 0] * spacing[:, 1] * 0.25
    return (area[:, None, None] * weights[:, None] * weights[None, :])[:, None, None, :, :, None]


def along_first(matrix, values):
    return jnp.einsum("xa,ecpabm->ecpxbm", matrix, values, precision=exact_precision)


def along_second(matrix, values):
    return jnp.einsum("yb,ecpabm->ecpaym", matrix, values, precision=exact_precision)


def span_derivative(values, wave_num):
    return jnp.stack((-wave_num * values[:, :, 1], wave_num * values[:, :, 0]), axis=2)


def side_scales(spacing):
    scale_x = (2.0 / spacing[:, 0])[:, None, None, None, None, None]
    scale_y = (2.0 / spacing[:, 1])[:, None, None, None, None, None]
    return (scale_x, scale_y)


def viscous_term(values, spacing, weights, derivative, wave_num):
    quad_wts = quad_weights(spacing, weights)
    scale_x, scale_y = side_scales(spacing)
    grad_x = scale_x * along_first(derivative, values)
    grad_y = scale_y * along_second(derivative, values)
    lateral = scale_x * along_first(derivative.T, quad_wts * grad_x) + scale_y * along_second(
        derivative.T, quad_wts * grad_y
    )
    return -viscosity * (lateral + wave_num * wave_num * quad_wts * values)


def advect_term(pair_vals, spacing, weights, derivative, wave_num):
    quad_wts = quad_weights(spacing, weights)
    scale_x, scale_y = side_scales(spacing)
    flux_x = jnp.stack([pair_vals[:, pair_pos] for pair_pos in pair_index[0]], axis=1)
    flux_y = jnp.stack([pair_vals[:, pair_pos] for pair_pos in pair_index[1]], axis=1)
    flux_z = jnp.stack([pair_vals[:, pair_pos] for pair_pos in pair_index[2]], axis=1)
    lateral = scale_x * along_first(derivative.T, quad_wts * flux_x) + scale_y * along_second(
        derivative.T, quad_wts * flux_y
    )
    return lateral - quad_wts * span_derivative(flux_z, wave_num)


def pair_cotangent(psi_vals, spacing, weights, derivative, wave_num):
    quad_wts = quad_weights(spacing, weights)
    scale_x, scale_y = side_scales(spacing)
    cot_table = (
        quad_wts * scale_x * along_first(derivative, psi_vals),
        quad_wts * scale_y * along_second(derivative, psi_vals),
        quad_wts * span_derivative(psi_vals, wave_num),
    )
    pair_list = [
        cot_table[left_idx][:, right_idx] + cot_table[right_idx][:, left_idx]
        for left_idx, right_idx in pair_order
    ]
    return jnp.stack(pair_list, axis=1)


def product_pairs(planes):
    return jnp.stack(
        [planes[:, left_idx] * planes[:, right_idx] for left_idx, right_idx in pair_order], axis=1
    )


def combine_pairs(spread_modes, planes):
    outputs = []
    for comp_idx in range(3):
        total = spread_modes[:, pair_index[comp_idx][0]] * planes[:, 0]
        total = total + spread_modes[:, pair_index[comp_idx][1]] * planes[:, 1]
        total = total + spread_modes[:, pair_index[comp_idx][2]] * planes[:, 2]
        outputs.append(total)
    return jnp.stack(outputs, axis=1)


def radial_sum(grid_vals, elem_axis, b_axis):
    layer_count = grid_vals.shape[b_axis]
    row_count = grid_vals.shape[elem_axis]
    top_layer = lax.slice_in_dim(grid_vals, layer_count - 1, layer_count, axis=b_axis)
    low_layer = lax.slice_in_dim(grid_vals, 0, 1, axis=b_axis)
    zero_row = jnp.zeros_like(lax.slice_in_dim(top_layer, 0, 1, axis=elem_axis))
    from_above = jnp.concatenate(
        (lax.slice_in_dim(low_layer, 1, row_count, axis=elem_axis), zero_row), axis=elem_axis
    )
    from_below = jnp.concatenate(
        (zero_row, lax.slice_in_dim(top_layer, 0, row_count - 1, axis=elem_axis)), axis=elem_axis
    )
    middle = lax.slice_in_dim(grid_vals, 1, layer_count - 1, axis=b_axis)
    return jnp.concatenate((low_layer + from_below, middle, top_layer + from_above), axis=b_axis)


def on_device(state, adjoint_end, observed, spacing, radial_slot):
    groups = lax.axis_size("modes")
    member = lax.axis_index("modes")
    elem_count = state.shape[0]
    local_modes = state.shape[4]
    total_modes = local_modes * groups
    weights_np, deriv_np = gll_tables(GLL)
    synth_np, analysis_np = fourier_tables(total_modes, 3 * total_modes)
    weights = jnp.asarray(weights_np, jnp.float32)
    derivative = jnp.asarray(deriv_np, jnp.float32)
    synthesis = jnp.asarray(synth_np, jnp.float32).astype(jnp.bfloat16)
    analysis_field = jnp.asarray(analysis_np, jnp.float32).astype(jnp.bfloat16)
    mode_ids = member * local_modes + jnp.arange(local_modes, dtype=jnp.int32)
    wave_local = wave_scale * mode_ids.astype(jnp.float32) / total_modes
    slot_row = radial_slot[0]
    onehot = (slot_row[:, None] == jnp.arange(elem_count, dtype=jnp.int32)[None, :]).astype(
        jnp.float32
    )
    wall_rows = (slot_row == 0).astype(jnp.float32)[:, None, None, None, None, None]
    wall_cols = (jnp.arange(GLL, dtype=jnp.int32) == 0).astype(jnp.float32)[
        None, None, None, None, :, None
    ]
    wall_mask = 1.0 - wall_rows * wall_cols
    quad_wts = quad_weights(spacing, weights)
    full_shape = (elem_count, 3, 2, GLL, GLL, local_modes)
    flat_shape = (elem_count, 3, 2, GLL * GLL, local_modes)
    values = state.reshape(full_shape)

    def assemble(element_vals):
        grid_vals = jnp.einsum("jr,jcpabm->rcpabm", onehot, element_vals, precision=exact_precision)
        grid_vals = radial_sum(grid_vals, 0, 4)
        widened = with_halo(grid_vals, (("elems", 3),), 1)
        first_layer = grid_vals[:, :, :, 0:1] + widened[:, :, :, 0:1]
        last_layer = grid_vals[:, :, :, GLL - 1 : GLL] + widened[:, :, :, GLL + 1 : GLL + 2]
        grid_vals = jnp.concatenate(
            (first_layer, grid_vals[:, :, :, 1 : GLL - 1], last_layer), axis=3
        )
        return jnp.einsum("jr,rcpabm->jcpabm", onehot, grid_vals, precision=exact_precision)

    mass = assemble(quad_wts)
    linear_part = quad_wts * values + time_step * viscous_term(
        values, spacing, weights, derivative, wave_local
    )
    state_low = state.astype(jnp.bfloat16)
    at_points = lax.all_to_all(state_low, "modes", split_axis=0, concat_axis=4, tiled=True)
    planes = jnp.einsum("ecpnm,pmq->ecnq", at_points, synthesis, preferred_element_type=jnp.float32)
    pair_physical_values = product_pairs(planes).astype(jnp.bfloat16)
    pair_spectral_coefficients = jnp.einsum(
        "abry,yuw->aburw", pair_physical_values, analysis_field, preferred_element_type=jnp.float32
    ).astype(jnp.bfloat16)
    pair_here = lax.all_to_all(
        pair_spectral_coefficients, "modes", split_axis=4, concat_axis=0, tiled=True
    )
    pair_here = pair_here.reshape(elem_count, 6, 2, GLL, GLL, local_modes).astype(jnp.float32)
    advect = advect_term(pair_here, spacing, weights, derivative, wave_local).astype(jnp.bfloat16)
    numerator_sum = assemble(linear_part + time_step * advect.astype(jnp.float32))
    next_state = wall_mask * numerator_sum / mass
    forcing = adjoint_end.reshape(full_shape) + (
        next_state - observed.reshape(full_shape).astype(jnp.float32)
    )
    psi_field = assemble(wall_mask * forcing / mass)
    psi_low = psi_field.astype(jnp.bfloat16)
    pair_adjoint_values = pair_cotangent(
        psi_low.astype(jnp.float32), spacing, weights, derivative, wave_local
    ).astype(jnp.bfloat16)
    spread_input = lax.all_to_all(
        pair_adjoint_values.reshape(elem_count, 6, 2, GLL * GLL, local_modes),
        "modes",
        split_axis=0,
        concat_axis=4,
        tiled=True,
    )
    spread_modes = jnp.einsum(
        "voyjg,zyg->vojz", spread_input, analysis_field, preferred_element_type=jnp.float32
    )
    planes_cot = combine_pairs(spread_modes, planes).astype(jnp.bfloat16)
    adjoint_adv = jnp.einsum(
        "ecnq,pmq->ecpnm", planes_cot, synthesis, preferred_element_type=jnp.float32
    ).astype(jnp.bfloat16)
    adjoint_here = lax.all_to_all(
        adjoint_adv, "modes", split_axis=4, concat_axis=0, tiled=True
    ).reshape(full_shape)
    viscous_adj = viscous_term(psi_field, spacing, weights, derivative, wave_local)
    adjoint_start = quad_wts * psi_field + time_step * (
        viscous_adj + adjoint_here.astype(jnp.float32)
    )
    return (next_state.reshape(flat_shape), adjoint_start.reshape(flat_shape))


def solution(mesh):
    in_specs = (
        P("elems", None, None, None, "modes"),
        P("elems", None, None, None, "modes"),
        P("elems", None, None, None, "modes"),
        P("elems", None),
        P("elems", None),
    )
    out_specs = (P("elems", None, None, None, "modes"), P("elems", None, None, None, "modes"))
    return jax.shard_map(
        on_device, mesh=mesh, in_specs=in_specs, out_specs=out_specs, check_vma=False
    )
```

profile of v0, /device:TPU:1, one launch (start us, length us, event | category | flops | bytes accessed | tf_op | source)
XLA Modules:
  0.0 185.3 jit_solution(5595633022089034657)
XLA Ops:
  0.7 2.0 %convert_element_type.117 = bf16[4,3,2,64,128]{4,3,2,1,0:T(8,128)(2,1)} convert(f32[4,3,2,64,128]{4,3,2,1,0:T(8,128)} %param.9) | non-fusion elementwise | flops 196608 | bytes 1179648 | tf_op jit(solution)/shard_map/convert_element_type | solution.py:205
  2.6 5.4 %all-to-all-start = ((bf16[4,3,2,64,128]{4,3,2,1,0:T(8,128)(2,1)}), bf16[4,3,2,64,128]{4,3,2,1,0:T(8,128)(2,1)S(1)}, u32[]{:S(2)}, u32[]{:S(2)}) async-start(bf16[4,3,2,64,128]{4,3,2,1,0:T(8,128)(2,1)} %convert_element_type.117), calls=%async_computation | async-start | bytes 786432 | tf_op jit(solution)/shard_map/all_to_all | solution.py:206
  8.2 0.7 multiply_multiply_fusion.1
  9.4 0.7 pad_maximum_fusion.4
  10.1 3.9 %collective-permute-start.2 = (f32[4,1,1,1,8,1]{4,0,3,5,2,1:T(4,128)}, f32[4,1,1,1,8,1]{4,0,3,5,2,1:T(4,128)}, u32[]{:S(2)}, u32[]{:S(2)}) collective-permute-start(f32[4,1,1,1,8,1]{4,0,3,5,2,1:T(4,128)} %pad_maximum_fusion.4), channel_id=1, source_target_pairs={{0,1},{1,2},{2,3},{3,4},{4,5},{5,6},{6,7},{7,8},{8,9},{9,10},{10,1... | collective-permute-start | bytes 392 | tf_op jit(solution)/shard_map/ppermute | solution.py:24
  14.1 0.5 compare_convert_fusion
  14.7 0.6 compare_convert_fusion.1
  15.2 0.8 broadcast_multiply_fusion
  16.5 2.7 %convolution_bitcast_fusion.1 = f32[1,3,64,1536]{3,2,1,0:T(8,128)S(1)} fusion(bf16[2,512,1536,1]{2,1,0,3:T(8,128)(2,1)} %constant.63, bf16[3,2,64,512]{3,2,1,0:T(8,128)(2,1)S(1)} %reshape.328), kind=kOutput, calls=%fused_computation.1 | convolution fusion | flops 603979776 | bytes 4718592 | tf_op jit(solution)/shard_map/ecpnm,pmq->ecnq/dot_general | solution.py:207
  19.4 1.7 copy-done.47
  21.1 1.4 fusion
  22.5 1.6 copy.180
  24.0 2.4 %reshape.357 = bf16[4,2,49152]{2,1,0:T(2,128)(2,1)} reshape(bf16[512,1,6,2,64]{4,3,2,1,0:T(2,128)(2,1)S(1)} %bitcast.236) | data formatting | bytes 1572864
  26.4 4.9 %all-to-all-start.1 = ((bf16[4,2,49152]{2,1,0:T(2,128)(2,1)}), bf16[4,2,49152]{2,1,0:T(2,128)(2,1)}, u32[]{:S(2)}, u32[]{:S(2)}) async-start(bf16[4,2,49152]{2,1,0:T(2,128)(2,1)} %reshape.357), calls=%async_computation.1 | async-start | bytes 1572864 | tf_op jit(solution)/shard_map/all_to_all | solution.py:212
  31.4 0.7 multiply_subtract_fusion
  32.1 1.4 copy.197
  33.5 0.6 convert_multiply_fusion
  34.1 0.8 fusion.140
  35.1 1.8 fusion.59
  36.9 1.7 fusion.6
  38.6 8.0 %all-to-all-done.1 = bf16[4,2,49152]{2,1,0:T(2,128)(2,1)} async-done(((bf16[4,2,49152]{2,1,0:T(2,128)(2,1)}), bf16[4,2,49152]{2,1,0:T(2,128)(2,1)}, u32[]{:S(2)}, u32[]{:S(2)}) %all-to-all-start.1) | async-done | bytes 786464 | tf_op jit(solution)/shard_map/all_to_all | solution.py:212
  46.6 2.8 %reshape.358 = bf16[512,1,6,2,64]{4,3,2,1,0:T(2,128)(2,1)S(1)} reshape(bf16[4,2,49152]{2,1,0:T(2,128)(2,1)} %all-to-all-done.1) | data formatting | bytes 1572864
  49.3 3.8 %copy.181 = f32[1,6,2,64,512]{4,0,3,2,1:T(1,128)} copy(bf16[1,6,2,64,512]{3,2,1,0,4:T(2,128)(2,1)S(1)} %bitcast.237) | data formatting | bytes 2359296 | tf_op jit(solution)/shard_map/convert_element_type | solution.py:215
  53.1 1.6 copy.316
  55.3 0.5 copy-done.10
  55.7 0.9 fusion.57
  57.4 1.1 fusion.25
  58.7 1.2 fusion.11
  59.9 1.5 fusion.55
  61.7 11.3 %collective-permute-start = (f32[4,3,2,1,8,128]{5,0,4,3,2,1:T(4,128)S(1)}, f32[4,3,2,1,8,128]{5,0,4,3,2,1:T(4,128)S(1)}, u32[]{:S(2)}, u32[]{:S(2)}) collective-permute-start(f32[4,3,2,1,8,128]{5,0,4,3,2,1:T(4,128)S(1)} %pad_maximum_fusion.2), channel_id=1, source_target_pairs={{0,1},{1,2},{2,3},{3,4},{4,5},{5,6},{6,7},{7,8},{8,9},{9,10},{10,1... | collective-permute-start | bytes 294920 | tf_op jit(solution)/shard_map/ppermute | solution.py:24
  73.0 0.7 fusion.150
  73.7 2.0 %collective-permute-start.3 = (f32[4,1,1,1,8,1]{4,0,3,5,2,1:T(4,128)S(1)}, f32[4,1,1,1,8,1]{4,0,3,5,2,1:T(4,128)S(1)}, u32[]{:S(2)}, u32[]{:S(2)}) collective-permute-start(f32[4,1,1,1,8,1]{4,0,3,5,2,1:T(4,128)S(1)} %get-tuple-element.17), channel_id=1, source_target_pairs={{1,0},{2,1},{3,2},{4,3},{5,4},{6,5},{7,6},{8,7},{9,8},{10,9},{11,1... | collective-permute-start | bytes 392 | tf_op jit(solution)/shard_map/ppermute | solution.py:27
  76.1 2.7 %collective-permute-done.3 = f32[4,1,1,1,8,1]{4,0,3,5,2,1:T(4,128)S(1)} collective-permute-done((f32[4,1,1,1,8,1]{4,0,3,5,2,1:T(4,128)S(1)}, f32[4,1,1,1,8,1]{4,0,3,5,2,1:T(4,128)S(1)}, u32[]{:S(2)}, u32[]{:S(2)}) %collective-permute-start.3) | collective-permute-done | bytes 160 | tf_op jit(solution)/shard_map/ppermute | solution.py:27
  78.8 0.7 add.169
  79.5 13.7 %collective-permute-start.1 = (f32[4,3,2,1,8,128]{5,0,4,3,2,1:T(4,128)S(1)}, f32[4,3,2,1,8,128]{5,0,4,3,2,1:T(4,128)S(1)}, u32[]{:S(2)}, u32[]{:S(2)}) collective-permute-start(f32[4,3,2,1,8,128]{5,0,4,3,2,1:T(4,128)S(1)} %get-tuple-element.19), channel_id=1, source_target_pairs={{1,0},{2,1},{3,2},{4,3},{5,4},{6,5},{7,6},{8,7},{9,8},{10,9},{11,1... | collective-permute-start | bytes 294920 | tf_op jit(solution)/shard_map/ppermute | solution.py:27
  93.9 1.0 fusion.22
  95.1 1.3 fusion.62
  96.7 1.9 %collective-permute-start.4 = (f32[4,3,2,1,8,128]{5,0,4,3,2,1:T(4,128)S(1)}, f32[4,3,2,1,8,128]{5,0,4,3,2,1:T(4,128)S(1)}, u32[]{:S(2)}, u32[]{:S(2)}) collective-permute-start(f32[4,3,2,1,8,128]{5,0,4,3,2,1:T(4,128)S(1)} %pad_maximum_fusion), channel_id=1, source_target_pairs={{0,1},{1,2},{2,3},{3,4},{4,5},{5,6},{6,7},{7,8},{8,9},{9,10},{10,1... | collective-permute-start | bytes 294920 | tf_op jit(solution)/shard_map/ppermute | solution.py:24
  98.6 11.9 %collective-permute-done.4 = f32[4,3,2,1,8,128]{5,0,4,3,2,1:T(4,128)S(1)} collective-permute-done((f32[4,3,2,1,8,128]{5,0,4,3,2,1:T(4,128)S(1)}, f32[4,3,2,1,8,128]{5,0,4,3,2,1:T(4,128)S(1)}, u32[]{:S(2)}, u32[]{:S(2)}) %collective-permute-start.4) | collective-permute-done | bytes 98336 | tf_op jit(solution)/shard_map/ppermute | solution.py:24
  110.5 13.9 %collective-permute-start.5 = (f32[4,3,2,1,8,128]{5,0,4,3,2,1:T(4,128)S(1)}, f32[4,3,2,1,8,128]{5,0,4,3,2,1:T(4,128)S(1)}, u32[]{:S(2)}, u32[]{:S(2)}) collective-permute-start(f32[4,3,2,1,8,128]{5,0,4,3,2,1:T(4,128)S(1)} %get-tuple-element.15), channel_id=1, source_target_pairs={{1,0},{2,1},{3,2},{4,3},{5,4},{6,5},{7,6},{8,7},{9,8},{10,9},{11,1... | collective-permute-start | bytes 294920 | tf_op jit(solution)/shard_map/ppermute | solution.py:27
  124.6 0.8 collective-permute-done.5
  125.4 1.0 fusion.30
  126.4 0.5 fusion.148
  127.1 0.5 copy-done.11
  129.4 1.0 copy.220
  130.4 3.6 %all-to-all-start.2 = ((bf16[4,6,2,64,128]{4,3,2,1,0:T(8,128)(2,1)}), bf16[4,6,2,64,128]{4,3,2,1,0:T(8,128)(2,1)S(1)}, u32[]{:S(2)}, u32[]{:S(2)}) async-start(bf16[4,6,2,64,128]{4,3,2,1,0:T(8,128)(2,1)} %copy.220), calls=%async_computation.2 | async-start | bytes 1572864 | tf_op jit(solution)/shard_map/all_to_all | solution.py:227
  134.1 1.0 copy.227
  135.1 0.8 fusion.53
  135.9 17.8 %all-to-all-done.2 = bf16[4,6,2,64,128]{4,3,2,1,0:T(8,128)(2,1)S(1)} async-done(((bf16[4,6,2,64,128]{4,3,2,1,0:T(8,128)(2,1)}), bf16[4,6,2,64,128]{4,3,2,1,0:T(8,128)(2,1)S(1)}, u32[]{:S(2)}, u32[]{:S(2)}) %all-to-all-start.2) | async-done | bytes 786464 | tf_op jit(solution)/shard_map/all_to_all | solution.py:227
  153.6 1.5 copy.221
  155.1 1.6 reshape.332
  156.8 3.3 %convolution_bitcast_fusion = f32[1,6,64,1536]{3,2,1,0:T(8,128)S(1)} fusion(bf16[6,2,64,512]{3,2,1,0:T(8,128)(2,1)S(1)} %reshape.332, bf16[1536,2,512,1]{2,0,1,3:T(8,128)(2,1)} %constant.64), kind=kOutput, calls=%fused_computation | convolution fusion | flops 1207959552 | bytes 6291456 | tf_op jit(solution)/shard_map/voyjg,zyg->vojz/dot_general | solution.py:234
  160.5 1.5 copy-done.46
  162.0 1.2 fusion.26
  163.2 1.1 copy.222
  164.3 1.3 reshape.359
  165.6 3.9 %all-to-all-start.3 = ((bf16[4,2,24576]{2,1,0:T(2,128)(2,1)}), bf16[4,2,24576]{2,1,0:T(2,128)(2,1)S(1)}, u32[]{:S(2)}, u32[]{:S(2)}) async-start(bf16[4,2,24576]{2,1,0:T(2,128)(2,1)} %reshape.359), calls=%async_computation.3 | async-start | bytes 786432 | tf_op jit(solution)/shard_map/all_to_all | solution.py:241
  169.7 0.9 fusion.49
  170.6 1.2 fusion.14
  171.9 7.1 %all-to-all-done.3 = bf16[4,2,24576]{2,1,0:T(2,128)(2,1)S(1)} async-done(((bf16[4,2,24576]{2,1,0:T(2,128)(2,1)}), bf16[4,2,24576]{2,1,0:T(2,128)(2,1)S(1)}, u32[]{:S(2)}, u32[]{:S(2)}) %all-to-all-start.3) | async-done | bytes 393248 | tf_op jit(solution)/shard_map/all_to_all | solution.py:241
  179.0 0.5 reshape.360
  179.5 1.8 copy.223
  181.4 2.9 %fusion.20 = f32[4,3,2,8,8,128]{5,3,4,2,1,0:T(8,128)S(1)} fusion(f32[4,3,2,8,8,128]{5,3,4,2,1,0:T(8,128)S(1)} %fusion.14, f32[8,8,1,1,1,1]{1,0,5,4,3,2:T(8,128)S(1)} %copy-done.14, f32[4,3,2,8,8,128]{5,0,4,3,2,1:T(4,128)} %bitcast.242, f32[4,3,2,8,128,8]{4,5,3,2,1,0:T(8,128)S(1)} %fusion.49, f32[4,3,2,8,8,128]{5,0,4,3,2,1:T(4,128)S(1)} %fusion.30, ...), kind=kOutput, calls=%fused_computation.29 | convolution fusion | flops 20840448 | bytes 4064544 | tf_op jit(solution)/shard_map/xa,ecpabm->ecpxbm/dot_general | solution.py:75
  184.3 1.0 copy.317
  (152 shorter events, 7.5 us)
Async XLA Ops:
  0.6 7.5 %copy-start.39 = (f32[8]{0:T(128)S(1)}, f32[8]{0:T(128)}, u32[]{:S(2)}) copy-start(f32[8]{0:T(128)} %constant.39.clone) | copy-start | bytes 100
  0.6 7.4 %copy-start.40 = (f32[4,2]{0,1:T(2,128)S(1)}, f32[4,2]{0,1:T(2,128)}, u32[]{:S(2)}) copy-start(f32[4,2]{0,1:T(2,128)} %param.12) | copy-start | bytes 100
  0.7 8.2 %copy-start.41 = (s32[1,4]{1,0:T(1,128)S(1)}, s32[1,4]{1,0:T(1,128)}, u32[]{:S(2)}) copy-start(s32[1,4]{1,0:T(1,128)} %param.13) | copy-start | bytes 52
  2.6 13.4 %all-to-all-start = ((bf16[4,3,2,64,128]{4,3,2,1,0:T(8,128)(2,1)}), bf16[4,3,2,64,128]{4,3,2,1,0:T(8,128)(2,1)S(1)}, u32[]{:S(2)}, u32[]{:S(2)}) async-start(bf16[4,3,2,64,128]{4,3,2,1,0:T(8,128)(2,1)} %convert_element_type.117), calls=%async_computation | async-start | bytes 786432 | tf_op jit(solution)/shard_map/all_to_all | solution.py:206
  8.1 0.8 copy-start.24
  8.1 0.8 copy-start.29
  9.3 4.7 %copy-start.16 = (f32[4,1,1,8,6,1]{4,0,3,5,2,1:T(4,128)}, f32[4,1,1,8,6,1]{4,0,3,5,2,1:T(4,128)S(1)}, u32[]{:S(2)}) copy-start(f32[4,1,1,8,6,1]{4,0,3,5,2,1:T(4,128)S(1)} %slice.288) | copy-start | bytes 2308
  9.4 4.7 %copy-start.18 = (f32[4,1,1,8,1,1]{4,0,3,5,2,1:T(4,128)}, f32[4,1,1,8,1,1]{4,0,3,5,2,1:T(4,128)S(1)}, u32[]{:S(2)}) copy-start(f32[4,1,1,8,1,1]{4,0,3,5,2,1:T(4,128)S(1)} %get-tuple-element.45) | copy-start | bytes 388
  9.4 4.7 %copy-start.20 = (f32[4,1,1,8,1,1]{4,0,3,5,2,1:T(4,128)}, f32[4,1,1,8,1,1]{4,0,3,5,2,1:T(4,128)S(1)}, u32[]{:S(2)}) copy-start(f32[4,1,1,8,1,1]{4,0,3,5,2,1:T(4,128)S(1)} %get-tuple-element.46) | copy-start | bytes 388
  10.1 62.9 %collective-permute-start.2 = (f32[4,1,1,1,8,1]{4,0,3,5,2,1:T(4,128)}, f32[4,1,1,1,8,1]{4,0,3,5,2,1:T(4,128)}, u32[]{:S(2)}, u32[]{:S(2)}) collective-permute-start(f32[4,1,1,1,8,1]{4,0,3,5,2,1:T(4,128)} %pad_maximum_fusion.4), channel_id=1, source_target_pairs={{0,1},{1,2},{2,3},{3,4},{4,5},{5,6},{6,7},{7,8},{8,9},{9,10},{10,1... | collective-permute-start | bytes 392 | tf_op jit(solution)/shard_map/ppermute | solution.py:24
  19.2 1.9 %copy-start.47 = (bf16[1536,2,512,1]{2,0,1,3:T(8,128)(2,1)S(1)}, bf16[1536,2,512,1]{2,0,1,3:T(8,128)(2,1)}, u32[]{:S(2)}) copy-start(bf16[1536,2,512,1]{2,0,1,3:T(8,128)(2,1)} %constant.64) | copy-start | bytes 9437188
  26.4 5.0 %copy-start.44 = (f32[8]{0:T(128)S(1)}, f32[8]{0:T(128)}, u32[]{:S(2)}) copy-start(f32[8]{0:T(128)} %compare_convert_fusion) | copy-start | bytes 100
  26.4 5.0 %copy-start.45 = (f32[4]{0:T(128)S(1)}, f32[4]{0:T(128)}, u32[]{:S(2)}) copy-start(f32[4]{0:T(128)} %compare_convert_fusion.1) | copy-start | bytes 52
  26.4 5.6 %copy-start.5 = (f32[4,3,2,64,128]{4,3,2,1,0:T(8,128)S(1)}, f32[4,3,2,64,128]{4,3,2,1,0:T(8,128)}, u32[]{:S(2)}) copy-start(f32[4,3,2,64,128]{4,3,2,1,0:T(8,128)} %param.10) | copy-start | bytes 2359300
  26.4 20.1 %all-to-all-start.1 = ((bf16[4,2,49152]{2,1,0:T(2,128)(2,1)}), bf16[4,2,49152]{2,1,0:T(2,128)(2,1)}, u32[]{:S(2)}, u32[]{:S(2)}) async-start(bf16[4,2,49152]{2,1,0:T(2,128)(2,1)} %reshape.357), calls=%async_computation.1 | async-start | bytes 1572864 | tf_op jit(solution)/shard_map/all_to_all | solution.py:212
  31.4 2.7 %copy-start = (f32[4,3,2,64,128]{4,3,2,1,0:T(8,128)S(1)}, f32[4,3,2,64,128]{4,3,2,1,0:T(8,128)}, u32[]{:S(2)}) copy-start(f32[4,3,2,64,128]{4,3,2,1,0:T(8,128)} %param.9) | copy-start | bytes 2359300
  31.4 2.7 %copy-start.9 = (f32[8,8,1,1,1,1]{1,0,5,4,3,2:T(8,128)S(1)}, f32[8,8,1,1,1,1]{1,0,5,4,3,2:T(8,128)}, u32[]{:S(2)}) copy-start(f32[8,8,1,1,1,1]{1,0,5,4,3,2:T(8,128)} %constant.62) | copy-start | bytes 772
  33.5 1.4 copy-start.30
  35.1 1.8 copy-start.25
  55.0 0.7 copy-start.10
  56.6 0.6 copy-start.35
  56.6 0.7 copy-start.37
  56.7 0.7 copy-start.26
  56.7 0.7 copy-start.31
  57.4 1.2 copy-start.1
  57.4 1.4 copy-start.2
  57.4 1.4 copy-start.3
  58.7 1.2 copy-start.42
  61.5 11.5 %copy-start.17 = (f32[4,1,1,8,6,1]{4,0,3,5,2,1:T(4,128)S(1)}, f32[4,1,1,8,6,1]{4,0,3,5,2,1:T(4,128)}, u32[]{:S(2)}) copy-start(f32[4,1,1,8,6,1]{4,0,3,5,2,1:T(4,128)} %copy-done.16) | copy-start | bytes 2308
  61.5 11.5 %copy-start.19 = (f32[4,1,1,8,1,1]{4,0,3,5,2,1:T(4,128)S(1)}, f32[4,1,1,8,1,1]{4,0,3,5,2,1:T(4,128)}, u32[]{:S(2)}) copy-start(f32[4,1,1,8,1,1]{4,0,3,5,2,1:T(4,128)} %copy-done.18) | copy-start | bytes 388
  61.5 11.5 %copy-start.21 = (f32[4,1,1,8,1,1]{4,0,3,5,2,1:T(4,128)S(1)}, f32[4,1,1,8,1,1]{4,0,3,5,2,1:T(4,128)}, u32[]{:S(2)}) copy-start(f32[4,1,1,8,1,1]{4,0,3,5,2,1:T(4,128)} %copy-done.20) | copy-start | bytes 388
  61.5 14.3 %copy-start.15 = (bf16[4,3,2,64,128]{4,3,2,1,0:T(8,128)(2,1)S(1)}, bf16[4,3,2,64,128]{4,3,2,1,0:T(8,128)(2,1)}, u32[]{:S(2)}) copy-start(bf16[4,3,2,64,128]{4,3,2,1,0:T(8,128)(2,1)} %param.11) | copy-start | bytes 1179652
  61.7 17.8 %collective-permute-start = (f32[4,3,2,1,8,128]{5,0,4,3,2,1:T(4,128)S(1)}, f32[4,3,2,1,8,128]{5,0,4,3,2,1:T(4,128)S(1)}, u32[]{:S(2)}, u32[]{:S(2)}) collective-permute-start(f32[4,3,2,1,8,128]{5,0,4,3,2,1:T(4,128)S(1)} %pad_maximum_fusion.2), channel_id=1, source_target_pairs={{0,1},{1,2},{2,3},{3,4},{4,5},{5,6},{6,7},{7,8},{8,9},{9,10},{10,1... | collective-permute-start | bytes 294920 | tf_op jit(solution)/shard_map/ppermute | solution.py:24
  73.7 20.2 %copy-start.34 = (f32[4,8]{0,1:T(8,128)S(1)}, f32[4,8]{0,1:T(8,128)}, u32[]{:S(2)}) copy-start(f32[4,8]{0,1:T(8,128)} %multiply_subtract_fusion) | copy-start | bytes 388
  73.7 5.0 %collective-permute-start.3 = (f32[4,1,1,1,8,1]{4,0,3,5,2,1:T(4,128)S(1)}, f32[4,1,1,1,8,1]{4,0,3,5,2,1:T(4,128)S(1)}, u32[]{:S(2)}, u32[]{:S(2)}) collective-permute-start(f32[4,1,1,1,8,1]{4,0,3,5,2,1:T(4,128)S(1)} %get-tuple-element.17), channel_id=1, source_target_pairs={{1,0},{2,1},{3,2},{4,3},{5,4},{6,5},{7,6},{8,7},{9,8},{10,9},{11,1... | collective-permute-start | bytes 392 | tf_op jit(solution)/shard_map/ppermute | solution.py:27
  79.5 14.4 %collective-permute-start.1 = (f32[4,3,2,1,8,128]{5,0,4,3,2,1:T(4,128)S(1)}, f32[4,3,2,1,8,128]{5,0,4,3,2,1:T(4,128)S(1)}, u32[]{:S(2)}, u32[]{:S(2)}) collective-permute-start(f32[4,3,2,1,8,128]{5,0,4,3,2,1:T(4,128)S(1)} %get-tuple-element.19), channel_id=1, source_target_pairs={{1,0},{2,1},{3,2},{4,3},{5,4},{6,5},{7,6},{8,7},{9,8},{10,9},{11,1... | collective-permute-start | bytes 294920 | tf_op jit(solution)/shard_map/ppermute | solution.py:27
  93.9 1.1 copy-start.6
  95.0 1.4 copy-start.7
  96.5 27.9 %copy-start.23 = (f32[4,8,8]{2,1,0:T(8,128)S(1)}, f32[4,8,8]{2,1,0:T(8,128)}, u32[]{:S(2)}) copy-start(f32[4,8,8]{2,1,0:T(8,128)} %get-tuple-element.49) | copy-start | bytes 3076
  96.6 28.0 %copy-start.22 = (f32[4,8,8]{2,1,0:T(8,128)S(1)}, f32[4,8,8]{2,1,0:T(8,128)}, u32[]{:S(2)}) copy-start(f32[4,8,8]{2,1,0:T(8,128)} %get-tuple-element.50) | copy-start | bytes 3076
  96.7 28.8 %copy-start.43 = (s32[1,4]{1,0:T(1,128)S(1)}, s32[1,4]{1,0:T(1,128)}, u32[]{:S(2)}) copy-start(s32[1,4]{1,0:T(1,128)} %param.13) | copy-start | bytes 52
  96.7 13.8 %collective-permute-start.4 = (f32[4,3,2,1,8,128]{5,0,4,3,2,1:T(4,128)S(1)}, f32[4,3,2,1,8,128]{5,0,4,3,2,1:T(4,128)S(1)}, u32[]{:S(2)}, u32[]{:S(2)}) collective-permute-start(f32[4,3,2,1,8,128]{5,0,4,3,2,1:T(4,128)S(1)} %pad_maximum_fusion), channel_id=1, source_target_pairs={{0,1},{1,2},{2,3},{3,4},{4,5},{5,6},{6,7},{7,8},{8,9},{9,10},{10,1... | collective-permute-start | bytes 294920 | tf_op jit(solution)/shard_map/ppermute | solution.py:24
  110.5 14.8 %collective-permute-start.5 = (f32[4,3,2,1,8,128]{5,0,4,3,2,1:T(4,128)S(1)}, f32[4,3,2,1,8,128]{5,0,4,3,2,1:T(4,128)S(1)}, u32[]{:S(2)}, u32[]{:S(2)}) collective-permute-start(f32[4,3,2,1,8,128]{5,0,4,3,2,1:T(4,128)S(1)} %get-tuple-element.15), channel_id=1, source_target_pairs={{1,0},{2,1},{3,2},{4,3},{5,4},{6,5},{7,6},{8,7},{9,8},{10,9},{11,1... | collective-permute-start | bytes 294920 | tf_op jit(solution)/shard_map/ppermute | solution.py:27
  126.4 0.6 copy-start.36
  126.4 0.7 copy-start.38
  126.9 0.7 copy-start.11
  130.4 3.6 %copy-start.8 = (f32[4,3,2,8,8,128]{5,0,4,3,2,1:T(4,128)S(1)}, f32[4,3,2,8,8,128]{5,0,4,3,2,1:T(4,128)}, u32[]{:S(2)}) copy-start(f32[4,3,2,8,8,128]{5,0,4,3,2,1:T(4,128)} %copy-done.7) | copy-start | bytes 2359300
  130.4 23.2 %all-to-all-start.2 = ((bf16[4,6,2,64,128]{4,3,2,1,0:T(8,128)(2,1)}), bf16[4,6,2,64,128]{4,3,2,1,0:T(8,128)(2,1)S(1)}, u32[]{:S(2)}, u32[]{:S(2)}) async-start(bf16[4,6,2,64,128]{4,3,2,1,0:T(8,128)(2,1)} %copy.220), calls=%async_computation.2 | async-start | bytes 1572864 | tf_op jit(solution)/shard_map/all_to_all | solution.py:227
  134.1 1.0 copy-start.12
  160.1 1.9 %copy-start.46 = (bf16[2,512,1536,1]{2,1,0,3:T(8,128)(2,1)S(1)}, bf16[2,512,1536,1]{2,1,0,3:T(8,128)(2,1)}, u32[]{:S(2)}) copy-start(bf16[2,512,1536,1]{2,1,0,3:T(8,128)(2,1)} %constant.63) | copy-start | bytes 9437188
  164.3 5.2 %copy-start.32 = (f32[4]{0:T(128)S(1)}, f32[4]{0:T(128)}, u32[]{:S(2)}) copy-start(f32[4]{0:T(128)} %copy-done.29) | copy-start | bytes 52
  165.6 4.1 %copy-start.13 = (f32[8,8,1,1,1,1]{1,0,5,4,3,2:T(8,128)S(1)}, f32[8,8,1,1,1,1]{1,0,5,4,3,2:T(8,128)}, u32[]{:S(2)}) copy-start(f32[8,8,1,1,1,1]{1,0,5,4,3,2:T(8,128)} %constant.62) | copy-start | bytes 772
  165.6 13.4 %all-to-all-start.3 = ((bf16[4,2,24576]{2,1,0:T(2,128)(2,1)}), bf16[4,2,24576]{2,1,0:T(2,128)(2,1)S(1)}, u32[]{:S(2)}, u32[]{:S(2)}) async-start(bf16[4,2,24576]{2,1,0:T(2,128)(2,1)} %reshape.359), calls=%async_computation.3 | async-start | bytes 786432 | tf_op jit(solution)/shard_map/all_to_all | solution.py:241
  169.7 0.9 copy-start.27
  179.5 1.9 %copy-start.4 = (f32[4,8,8,128]{3,1,2,0:T(8,128)S(1)}, f32[4,8,8,128]{3,1,2,0:T(8,128)}, u32[]{:S(2)}) copy-start(f32[4,8,8,128]{3,1,2,0:T(8,128)} %broadcast_multiply_fusion) | copy-start | bytes 393220
  179.5 1.9 %copy-start.14 = (f32[8,8,1,1,1,1]{1,0,5,4,3,2:T(8,128)S(1)}, f32[8,8,1,1,1,1]{1,0,5,4,3,2:T(8,128)}, u32[]{:S(2)}) copy-start(f32[8,8,1,1,1,1]{1,0,5,4,3,2:T(8,128)} %constant.62) | copy-start | bytes 772
  179.5 1.9 %copy-start.28 = (f32[4]{0:T(128)S(1)}, f32[4]{0:T(128)}, u32[]{:S(2)}) copy-start(f32[4]{0:T(128)} %copy-done.24) | copy-start | bytes 52
  179.5 1.9 %copy-start.33 = (f32[4]{0:T(128)S(1)}, f32[4]{0:T(128)}, u32[]{:S(2)}) copy-start(f32[4]{0:T(128)} %copy-done.29) | copy-start | bytes 52
where the time goes:
time: 186 us; the launch traced here: 185 us
  starting transfers between devices  64.6 us (35%)
  waiting for transfers between devices  48.6 us (26%)
  local copies, waits for them, and re-layouts  31.6 us (17%)
  matrix products  27.9 us (15%)
  other arithmetic  10.8 us (6%)
    ppermute x3, starting transfers between devices, with_halo(): lax.ppermute(lax.slice_in_dim(block, 0, width, axis=dim), axis, backward)  29.6 us
    all_to_all x1, waiting for transfers between devices, on_device(): lax.all_to_all(pair_adjoint_values.reshape(elem_count, 6, 2, GLL * GLL, l...  17.8 us
    ppermute x3, starting transfers between devices, with_halo(): lax.ppermute(lax.slice_in_dim(block, block.shape[dim] - width, None, axis...  17.2 us
    unnamed x110, local copies, waits for them, and re-layouts  14.9 us
    ppermute x3, waiting for transfers between devices, with_halo(): lax.ppermute(lax.slice_in_dim(block, block.shape[dim] - width, None, axis...  11.9 us
    dot_general x6, matrix products, along_first(): jnp.einsum('xa,ecpabm->ecpxbm', matrix, values, precision=exact_precision)  8.57 us
    all_to_all x1, waiting for transfers between devices, on_device(): lax.all_to_all(pair_spectral_coefficients, 'modes', split_axis=4, concat_...  8 us
    all_to_all x1, waiting for transfers between devices, on_device(): lax.all_to_all(adjoint_adv, 'modes', split_axis=4, concat_axis=0, tiled=T...  7.15 us
  transfers between devices with their start and end apart: 10, of which 7 were waited for; matrix products, arithmetic and copies ran while one was open for 21% of the time, Pallas kernels for 0%

commit v1 on v0

v1 whole, which is shorter than its diff:
```python
import jax
import jax.numpy as jnp
import numpy as np
from jax import lax
from jax.experimental import pallas as pl
from jax.experimental.pallas import tpu as pltpu
from jax.sharding import PartitionSpec as P

GLL = 8
NODES = GLL * GLL
ROWS = 4
time_step = 0.01
viscosity = 0.05
wave_scale = 4.0
pair_order = ((0, 0), (0, 1), (0, 2), (1, 1), (1, 2), (2, 2))
pair_index = ((0, 1, 2), (1, 3, 4), (2, 4, 5))
F32 = jnp.float32
LOW = jnp.bfloat16
MESH = pl.DeviceIdType.MESH


def legendre_table(points, quad_count):
    columns = [points * 0.0 + 1.0, points]
    for degree in range(2, quad_count):
        columns.append(
            ((2 * degree - 1) * points * columns[-1] - (degree - 1) * columns[-2]) / degree
        )
    return np.stack(columns, axis=1)


def gll_tables(quad_count):
    degree = quad_count - 1
    points = -np.cos(np.pi * np.arange(quad_count) / degree)
    for repeat in range(60):
        vander = legendre_table(points, quad_count)
        points = points - (points * vander[:, degree] - vander[:, degree - 1]) / (
            quad_count * vander[:, degree]
        )
    vander = legendre_table(points, quad_count)
    edge_value = vander[:, degree]
    weights = 2.0 / (degree * quad_count * edge_value * edge_value)
    diagonal_mask = np.arange(quad_count)[:, None] == np.arange(quad_count)[None, :]
    differ = np.where(diagonal_mask, 1.0, points[:, None] - points[None, :])
    derivative = np.where(diagonal_mask, 0.0, edge_value[:, None] / (edge_value[None, :] * differ))
    derivative[0, 0] = -degree * quad_count / 4.0
    derivative[degree, degree] = degree * quad_count / 4.0
    return (weights, derivative)


def half_tables(modes, planes):
    half = planes // 2
    turns = np.outer(np.arange(modes), 2 * np.arange(half) + 1) % (2 * planes)
    angles = np.pi * turns / planes
    factor = np.where(np.arange(modes) == 0, 1.0, 2.0)[:, None]
    synth = np.stack((factor * np.cos(angles), -factor * np.sin(angles)))
    analysis = np.stack((np.cos(angles), -np.sin(angles))) * (2.0 / planes)
    return synth, np.transpose(analysis, (0, 2, 1))


def node_tables():
    weights, deriv = gll_tables(GLL)
    wdiag = np.diag(weights)
    back = deriv.T @ wdiag
    ahead = wdiag @ deriv
    stiff = deriv.T @ wdiag @ deriv
    zero = np.zeros((NODES, NODES))
    fwd = (
        np.concatenate((np.kron(back, wdiag), np.kron(wdiag, back), np.kron(stiff, wdiag)), 1),
        np.concatenate((zero, zero, np.kron(wdiag, stiff)), 1),
    )
    adj = (
        np.concatenate((np.kron(ahead, wdiag), np.kron(wdiag, ahead), np.kron(stiff, wdiag)), 0),
        np.concatenate((zero, zero, np.kron(wdiag, stiff)), 0),
    )
    return np.stack(fwd), np.stack(adj), np.kron(weights, weights)


def step_kernel(
    groups,
    slabs,
    state_ref, adj_ref, obs_ref, spacing_ref, slot_ref, synth_ref, anal_ref, fwd_ref, bwd_ref, w2_ref,
    next_ref, start_ref,
    state_v, adj_v, obs_v, synth_v, anal_v, fwd_v, bwd_v, w2_v,
    send_v, state_r, forcing_r, next_r, start_r, quad_v, scale_v, mult_v,
    even_v, odd_v, prod_v, modal_v, num_v, psi_v, cot_v, spread_v, pcot_v,
    edge_send, edge_recv, mass_send, mass_recv, out_v,
    load_sem, send_sem, recv_sem, esend_sem, erecv_sem, msend_sem, mrecv_sem, out_sem,
):
    member = lax.axis_index("modes")
    slab = lax.axis_index("elems")
    low_slab = lax.rem(slab + slabs - 1, slabs)
    high_slab = lax.rem(slab + 1, slabs)
    partners = (lax.rem(member + 2, 4), 3 - member, member + 1 - 2 * lax.rem(member, 2))
    modes = groups * 128
    recv = (state_r, forcing_r, next_r, start_r)

    loads = [
        pltpu.make_async_copy(src, dst, load_sem.at[i])
        for i, (src, dst) in enumerate(
            (
                (state_ref, state_v), (adj_ref, adj_v), (obs_ref, obs_v), (w2_ref, w2_v),
                (fwd_ref, fwd_v), (synth_ref, synth_v), (anal_ref, anal_v), (bwd_ref, bwd_v),
            )
        )
    ]
    for load in loads:
        load.start()

    barrier = pltpu.get_barrier_semaphore()
    for partner in partners:
        pl.semaphore_signal(barrier, inc=1, device_id={"modes": partner}, device_id_type=MESH)
    for near in (low_slab, high_slab):
        pl.semaphore_signal(barrier, inc=1, device_id={"elems": near}, device_id_type=MESH)

    slots = [slot_ref[0, j] for j in range(ROWS)]

    def flat(block):
        return block.reshape(6 * NODES, 128)

    def elem_of(row):
        place = jnp.int32(0)
        for j in range(1, ROWS):
            place = jnp.where(slots[j] == row, j, place)
        return place

    def swap(phase, partner):
        return pltpu.make_async_remote_copy(
            src_ref=send_v.at[phase, partner],
            dst_ref=recv[phase].at[member],
            send_sem=send_sem.at[phase, partner],
            recv_sem=recv_sem.at[phase, member],
            device_id={"modes": partner},
            device_id_type=MESH,
        )

    def swapped(phase, partner):
        return pltpu.make_async_remote_copy(
            src_ref=send_v.at[phase, partner],
            dst_ref=recv[phase].at[partner],
            send_sem=send_sem.at[phase, partner],
            recv_sem=recv_sem.at[phase, partner],
            device_id={"modes": partner},
            device_id_type=MESH,
        )

    loads[0].wait()
    pl.semaphore_wait(barrier, 5)
    for partner in partners:
        send_v[0, partner] = flat(state_v[elem_of(partner)]).astype(LOW)
        swap(0, partner).start()
    state_r[member] = flat(state_v[elem_of(member)]).astype(LOW)

    loads[3].wait()
    own = elem_of(member)
    above = elem_of(jnp.minimum(member + 1, ROWS - 1))
    below = elem_of(jnp.maximum(member - 1, 0))

    def area(elem):
        return spacing_ref[elem, 0] * spacing_ref[elem, 1] * 0.25

    side_x = spacing_ref[own, 0]
    side_y = spacing_ref[own, 1]
    full = (NODES, 128)
    layer = lax.rem(lax.broadcasted_iota(jnp.int32, full, 0), GLL)
    has_above = jnp.logical_and(layer == GLL - 1, member < ROWS - 1)
    has_below = jnp.logical_and(layer == 0, member > 0)
    w2 = w2_v[...]
    quad = w2 * area(own)
    quad_v[...] = quad
    mass = quad + jnp.where(has_above, w2 * area(above), 0.0)
    mass = mass + jnp.where(has_below, w2 * area(below), 0.0)
    scale_v[...] = mass
    mass_send[0] = mass[NODES - GLL :]
    mass_send[1] = mass[:GLL]

    def mass_copy(way):
        return pltpu.make_async_remote_copy(
            src_ref=mass_send.at[way],
            dst_ref=mass_recv.at[way],
            send_sem=msend_sem.at[way],
            recv_sem=mrecv_sem.at[way],
            device_id={"elems": (high_slab, low_slab)[way]},
            device_id_type=MESH,
        )

    mass_copy(0).start()
    mass_copy(1).start()
    copies = jnp.where(jnp.logical_or(has_above, has_below), 2.0, 1.0).astype(F32)
    node_a = lax.broadcasted_iota(jnp.int32, full, 0) // GLL
    mult_v[...] = jnp.where(jnp.logical_or(node_a == 0, node_a == GLL - 1), 2.0 * copies, copies)

    loads[1].wait()
    loads[2].wait()
    for partner in partners:
        elem = elem_of(partner)
        send_v[1, partner] = flat(adj_v[elem] - obs_v[elem].astype(F32)).astype(LOW)
    forcing_r[member] = flat(adj_v[own] - obs_v[own].astype(F32)).astype(LOW)

    mass_copy(0).wait()
    mass_copy(1).wait()
    scale_v[:GLL, :] = scale_v[:GLL, :] + mass_recv[0]
    scale_v[NODES - GLL :, :] = scale_v[NODES - GLL :, :] + mass_recv[1]
    at_wall = jnp.logical_and(layer == 0, member == 0)
    scale_v[...] = jnp.where(at_wall, 0.0, 1.0) / scale_v[...]

    loads[4].wait()
    loads[7].wait()
    lane = lax.broadcasted_iota(jnp.int32, (NODES, 3 * NODES), 1)
    ratio = jnp.full((NODES, 3 * NODES), side_y) / jnp.full((NODES, 3 * NODES), side_x)
    coef = jnp.where(
        lane < NODES, 0.5 * side_y, jnp.where(lane < 2 * NODES, 0.5 * side_x, -viscosity * ratio)
    )
    fwd_mat = (time_step * (fwd_v[0] * coef - fwd_v[1] * (viscosity / ratio))).astype(LOW)
    line = lax.broadcasted_iota(jnp.int32, (3 * NODES, NODES), 0)
    ratio = jnp.full((3 * NODES, NODES), side_y) / jnp.full((3 * NODES, NODES), side_x)
    coef = jnp.where(
        line < NODES, 0.5 * side_y, jnp.where(line < 2 * NODES, 0.5 * side_x, -viscosity * ratio)
    )
    bwd_mat = (bwd_v[0] * coef - bwd_v[1] * (viscosity / ratio)).astype(LOW)

    for partner in partners:
        swap(0, partner).wait_send()
        swap(1, partner).start()
    for partner in partners:
        swapped(0, partner).wait_recv()

    def rows_of(index, count=NODES):
        return pl.ds(index * count, count)

    def gathered(phase, i):
        return jnp.concatenate([recv[phase][q, rows_of(i), :] for q in range(groups)], axis=1)

    def wide(block):
        return jnp.concatenate([block] * groups, axis=1)

    def field(buf, i):
        return jnp.concatenate([buf[rows_of(6 * q + i), :] for q in range(groups)], axis=1)

    def set_field(buf, i, value):
        for q in range(groups):
            buf[rows_of(6 * q + i), :] = value[:, q * 128 : (q + 1) * 128]

    mode_ids = lax.broadcasted_iota(jnp.int32, (NODES, modes), 1)
    wave = mode_ids.astype(F32) * (wave_scale / modes)

    loads[5].wait()
    even_v[...] = jnp.dot(
        jnp.concatenate([gathered(0, 2 * c) for c in range(3)], axis=0),
        synth_v[0],
        preferred_element_type=F32,
    )
    odd_v[...] = jnp.dot(
        jnp.concatenate([gathered(0, 2 * c + 1) for c in range(3)], axis=0),
        synth_v[1],
        preferred_element_type=F32,
    )

    for q, (left, right) in enumerate(pair_order):
        el, ol = even_v[rows_of(left), :], odd_v[rows_of(left), :]
        er, orr = even_v[rows_of(right), :], odd_v[rows_of(right), :]
        prod_v[0, rows_of(q), :] = (el * er + ol * orr).astype(LOW)
        prod_v[1, rows_of(q), :] = (el * orr + ol * er).astype(LOW)
    loads[6].wait()
    for p in range(2):
        modal_v[p] = jnp.dot(prod_v[p], anal_v[p], preferred_element_type=F32).astype(LOW)

    for c in range(3):
        for p in range(2):
            values = gathered(0, 2 * c + p)
            stack = jnp.concatenate(
                [
                    modal_v[p, rows_of(pair_index[0][c]), :],
                    modal_v[p, rows_of(pair_index[1][c]), :],
                    values,
                ],
                axis=0,
            )
            flux_z = modal_v[1 - p, rows_of(pair_index[2][c]), :].astype(F32)
            turn = (-time_step if p == 1 else time_step) * wave
            local = (1.0 - time_step * viscosity * wave * wave) * values.astype(F32)
            set_field(
                num_v,
                2 * c + p,
                jnp.dot(fwd_mat, stack, preferred_element_type=F32)
                + wide(quad_v[...]) * (local + turn * flux_z),
            )

    edge_rows = 6 * GLL * groups

    def assemble(which, buf):
        def edge_copy(way):
            if way == 0:
                target = {"modes": jnp.minimum(member + 1, ROWS - 1)}
            elif way == 1:
                target = {"modes": jnp.maximum(member - 1, 0)}
            else:
                target = {"elems": (high_slab, low_slab)[way - 2]}
            return pltpu.make_async_remote_copy(
                src_ref=edge_send.at[which, way],
                dst_ref=edge_recv.at[which, way],
                send_sem=esend_sem.at[which, way],
                recv_sem=erecv_sem.at[which, way],
                device_id=target,
                device_id_type=MESH,
            )

        top = pl.ds(GLL - 1, edge_rows, stride=GLL)
        low = pl.ds(0, edge_rows, stride=GLL)

        @pl.when(member < ROWS - 1)
        def _():
            edge_send[which, 0] = buf[top, :].astype(LOW)
            edge_copy(0).start()

        @pl.when(member > 0)
        def _():
            edge_send[which, 1] = buf[low, :].astype(LOW)
            edge_copy(1).start()

        @pl.when(member > 0)
        def _():
            edge_copy(0).wait_recv()
            buf[low, :] = buf[low, :] + edge_recv[which, 0].astype(F32)

        @pl.when(member < ROWS - 1)
        def _():
            edge_copy(1).wait_recv()
            buf[top, :] = buf[top, :] + edge_recv[which, 1].astype(F32)

        for way, start in ((2, NODES - GLL), (3, 0)):
            edge_send[which, way] = jnp.concatenate(
                [buf[pl.ds(i * NODES + start, GLL), :] for i in range(6 * groups)], axis=0
            ).astype(LOW)
            edge_copy(way).start()
        for way, start in ((2, 0), (3, NODES - GLL)):
            edge_copy(way).wait_recv()
            came = edge_recv[which, way].astype(F32)
            for i in range(6 * groups):
                rows = pl.ds(i * NODES + start, GLL)
                buf[rows, :] = buf[rows, :] + came[i * GLL : (i + 1) * GLL]
        for way in (2, 3):
            edge_copy(way).wait_send()

        @pl.when(member < ROWS - 1)
        def _():
            edge_copy(0).wait_send()

        @pl.when(member > 0)
        def _():
            edge_copy(1).wait_send()

    assemble(0, num_v)
    for q in range(groups):
        for i in range(6):
            value = scale_v[...] * num_v[rows_of(6 * q + i), :]
            num_v[rows_of(6 * q + i), :] = value
            send_v[2, q, rows_of(i), :] = value.astype(LOW)
    for partner in partners:
        swap(1, partner).wait_send()
        swap(2, partner).start()
    next_r[member] = send_v[2, member]

    for partner in partners:
        swapped(1, partner).wait_recv()
    for q in range(groups):
        for i in range(6):
            psi_v[rows_of(6 * q + i), :] = scale_v[...] * forcing_r[q, rows_of(i), :].astype(F32)
    assemble(1, psi_v)
    for i in range(6 * groups):
        psi_v[rows_of(i), :] = psi_v[rows_of(i), :] + mult_v[...] * (
            scale_v[...] * num_v[rows_of(i), :]
        )

    norm = jnp.where(mode_ids == 0, 1.0 / (3.0 * modes), 0.5 / (3.0 * modes)).astype(F32)
    for p in range(2):
        lateral = []
        for c in range(3):
            psi = field(psi_v, 2 * c + p)
            other = field(psi_v, 2 * c + 1 - p)
            grads = jnp.dot(bwd_mat, psi.astype(LOW), preferred_element_type=F32)
            set_field(
                num_v,
                2 * c + p,
                wide(quad_v[...]) * ((1.0 - time_step * viscosity * wave * wave) * psi)
                + time_step * grads[2 * NODES :],
            )
            turn = -wave if p == 0 else wave
            lateral.append((grads[:NODES], grads[NODES : 2 * NODES], wide(quad_v[...]) * (turn * other)))
        for q, (left, right) in enumerate(pair_order):
            cot = lateral[right][left] + lateral[left][right]
            cot_v[p, rows_of(q), :] = (norm * cot).astype(LOW)

    for p in range(2):
        spread_v[p] = jnp.dot(cot_v[p], synth_v[p], preferred_element_type=F32)
    for c in range(3):
        even = jnp.zeros((NODES, even_v.shape[1]), F32)
        odd = jnp.zeros((NODES, even_v.shape[1]), F32)
        for d in range(3):
            se = spread_v[0, rows_of(pair_index[c][d]), :]
            so = spread_v[1, rows_of(pair_index[c][d]), :]
            ed, od = even_v[rows_of(d), :], odd_v[rows_of(d), :]
            even = even + (se * ed + so * od)
            odd = odd + (se * od + so * ed)
        pcot_v[0, rows_of(c), :] = even.astype(LOW)
        pcot_v[1, rows_of(c), :] = odd.astype(LOW)
    gain = jnp.where(mode_ids == 0, 3.0 * modes * time_step, 6.0 * modes * time_step).astype(F32)
    for p in range(2):
        back = jnp.dot(pcot_v[p], anal_v[p], preferred_element_type=F32)
        for c in range(3):
            low = (
                field(num_v, 2 * c + p) + gain * back[c * NODES : (c + 1) * NODES]
            ).astype(LOW)
            for q in range(groups):
                send_v[3, q, rows_of(2 * c + p), :] = low[:, q * 128 : (q + 1) * 128]
    for partner in partners:
        swap(2, partner).wait_send()
        swap(3, partner).start()
    start_r[member] = send_v[3, member]

    stores = []
    for which, target in ((0, next_ref), (1, start_ref)):
        for partner in partners:
            swapped(2 + which, partner).wait_recv()
        for j in range(ROWS):
            out_v[which, j] = recv[2 + which][slots[j]].astype(F32).reshape(3, 2, NODES, 128)
        store = pltpu.make_async_copy(out_v.at[which], target, out_sem.at[which])
        store.start()
        stores.append(store)
    for store in stores:
        store.wait()
    for partner in partners:
        swap(3, partner).wait_send()


def on_device(state, adjoint_end, observed, spacing, radial_slot):
    groups = lax.axis_size("modes")
    slabs = lax.axis_size("elems")
    modes = groups * state.shape[4]
    half = 3 * modes // 2
    synth, analysis = half_tables(modes, 3 * modes)
    fwd, bwd, w2 = node_tables()
    any_spec = pl.BlockSpec(memory_space=pl.ANY)
    smem_spec = pl.BlockSpec(memory_space=pltpu.SMEM)
    local = state.shape
    block = (6 * NODES, 128)
    vm = pltpu.VMEM
    sem = pltpu.SemaphoreType.DMA

    def run(*args):
        step_kernel(groups, slabs, *args)

    return pl.pallas_call(
        run,
        out_shape=(jax.ShapeDtypeStruct(local, F32), jax.ShapeDtypeStruct(local, F32)),
        in_specs=[any_spec] * 3 + [smem_spec] * 2 + [any_spec] * 5,
        out_specs=(any_spec, any_spec),
        scratch_shapes=[
            vm(local, F32), vm(local, F32), vm(local, LOW),
            vm((2, modes, half), LOW), vm((2, half, modes), LOW),
            vm((2, NODES, 3 * NODES), F32), vm((2, 3 * NODES, NODES), F32), vm((NODES, 128), F32),
            vm((4, ROWS) + block, LOW), *[vm((ROWS,) + block, LOW)] * 4,
            vm((NODES, 128), F32), vm((NODES, 128), F32), vm((NODES, 128), F32),
            vm((3 * NODES, half), F32), vm((3 * NODES, half), F32),
            vm((2, 6 * NODES, half), LOW), vm((2, 6 * NODES, modes), LOW),
            vm((6 * NODES * groups, 128), F32), vm((6 * NODES * groups, 128), F32),
            vm((2, 6 * NODES, modes), LOW), vm((2, 6 * NODES, half), F32),
            vm((2, 3 * NODES, half), LOW),
            vm((2, 4, 6 * GLL * groups, 128), LOW), vm((2, 4, 6 * GLL * groups, 128), LOW),
            vm((2, GLL, 128), F32), vm((2, GLL, 128), F32),
            vm((2,) + local, F32),
            sem((8,)), sem((4, ROWS)), sem((4, ROWS)), sem((2, 4)), sem((2, 4)),
            sem((2,)), sem((2,)), sem((2,)),
        ],
        compiler_params=pltpu.CompilerParams(
            collective_id=0, has_side_effects=True, vmem_limit_bytes=48 * 1024 * 1024
        ),
        cost_estimate=pl.CostEstimate(
            flops=1900000000, bytes_accessed=7000000, transcendentals=0
        ),
    )(
        state, adjoint_end, observed, spacing, radial_slot,
        jnp.asarray(synth, F32).astype(LOW), jnp.asarray(analysis, F32).astype(LOW),
        jnp.asarray(fwd, F32), jnp.asarray(bwd, F32),
        jnp.asarray(np.broadcast_to(w2[:, None], (NODES, 128)), F32),
    )


def solution(mesh):
    in_specs = (
        P("elems", None, None, None, "modes"),
        P("elems", None, None, None, "modes"),
        P("elems", None, None, None, "modes"),
        P("elems", None),
        P("elems", None),
    )
    out_specs = (P("elems", None, None, None, "modes"), P("elems", None, None, None, "modes"))
    return jax.shard_map(
        on_device, mesh=mesh, in_specs=in_specs, out_specs=out_specs, check_vma=False
    )
```

time: 186 us -> 75 us (0.40)
  the two profiles are of different devices: /device:TPU:1 before, /device:TPU:8 now
where the time goes in v1:
time: 75 us; the launch traced here: 74.6 us
  Pallas kernels  63.5 us (85%)
  local copies, waits for them, and re-layouts  10.4 us (14%)
    pallas_call x1, Pallas kernels, on_device(): pl.pallas_call(run, out_shape=(jax.ShapeDtypeStruct(local, F32), jax.Shap...  63.5 us
    unnamed x19, local copies, waits for them, and re-layouts  10.4 us

profile of v1, /device:TPU:8, one launch (start us, length us, event | category | flops | bytes accessed | tf_op | source)
XLA Modules:
  0.0 74.6 jit_solution(12296065314302186735)
XLA Ops:
  0.6 0.8 %copy.12.args_3_ = f32[4,2]{1,0:T(4,128)S(1)} copy(f32[4,2]{0,1:T(2,128)} %param.13) | data formatting | bytes 64 | tf_op args[3]
  1.4 0.0 copy-start
  1.4 1.1 %copy-done = f32[4,3,2,64,128]{4,3,2,1,0:T(8,128)S(1)} copy-done((f32[4,3,2,64,128]{4,3,2,1,0:T(8,128)S(1)}, f32[4,3,2,64,128]{4,3,2,1,0:T(8,128)}, u32[]{:S(2)}) %copy-start) | copy-done | bytes 786456
  2.5 0.0 copy-start.1
  2.5 1.1 %copy-done.1 = f32[4,3,2,64,128]{4,3,2,1,0:T(8,128)S(1)} copy-done((f32[4,3,2,64,128]{4,3,2,1,0:T(8,128)S(1)}, f32[4,3,2,64,128]{4,3,2,1,0:T(8,128)}, u32[]{:S(2)}) %copy-start.1) | copy-done | bytes 786456
  3.7 0.0 copy-start.2
  3.7 1.0 %copy-done.2 = bf16[4,3,2,64,128]{4,3,2,1,0:T(8,128)(2,1)S(1)} copy-done((bf16[4,3,2,64,128]{4,3,2,1,0:T(8,128)(2,1)S(1)}, bf16[4,3,2,64,128]{4,3,2,1,0:T(8,128)(2,1)}, u32[]{:S(2)}) %copy-start.2) | copy-done | bytes 393240
  4.7 0.0 copy-start.3
  4.7 0.7 copy-done.3
  5.3 0.0 copy-start.4
  5.3 1.4 %copy-done.4 = bf16[2,512,768]{2,1,0:T(8,128)(2,1)S(1)} copy-done((bf16[2,512,768]{2,1,0:T(8,128)(2,1)S(1)}, bf16[2,512,768]{2,1,0:T(8,128)(2,1)}, u32[]{:S(2)}) %copy-start.4) | copy-done | bytes 1572888
  6.7 0.0 copy-start.5
  6.7 0.9 %copy-done.5 = f32[2,192,64]{2,1,0:T(8,128)S(1)} copy-done((f32[2,192,64]{2,1,0:T(8,128)S(1)}, f32[2,192,64]{2,1,0:T(8,128)}, u32[]{:S(2)}) %copy-start.5) | copy-done | bytes 98328
  7.7 0.0 copy-start.6
  7.7 0.9 %copy-done.6 = f32[2,64,192]{2,1,0:T(8,128)S(1)} copy-done((f32[2,64,192]{2,1,0:T(8,128)S(1)}, f32[2,64,192]{2,1,0:T(8,128)}, u32[]{:S(2)}) %copy-start.6) | copy-done | bytes 98328
  8.6 0.0 copy-start.7
  8.6 0.8 %copy-done.7 = f32[64,128]{1,0:T(8,128)S(1)} copy-done((f32[64,128]{1,0:T(8,128)S(1)}, f32[64,128]{1,0:T(8,128)}, u32[]{:S(2)}) %copy-start.7) | copy-done | bytes 32792
  9.3 63.5 %shard_map.113 = (f32[4,3,2,64,128]{4,3,2,1,0:T(8,128)S(1)}, f32[4,3,2,64,128]{4,3,2,1,0:T(8,128)S(1)}) custom-call(f32[4,3,2,64,128]{4,3,2,1,0:T(8,128)S(1)} %copy-done, f32[4,3,2,64,128]{4,3,2,1,0:T(8,128)S(1)} %copy-done.1, bf16[4,3,2,64,128]{4,3,2,1,0:T(8,128)(2,1)S(1)} %copy-done.2, f32[4,2]{1,0:T(4,128)S(1)} %copy.12.args_3_, s32[1,4]{1,0:T(1,128)S(1)} %copy-done.3, ...), custom_call_target="tpu_custom_call" | custom-call | flops 1900000000 | bytes 7000000 | tf_op jit(solution)/shard_map/pallas_call | solution.py:452
  72.8 0.9 %copy.15 = f32[4,3,2,64,128]{4,3,2,1,0:T(8,128)} copy(f32[4,3,2,64,128]{4,3,2,1,0:T(8,128)S(1)} %get-tuple-element.4) | data formatting | bytes 1572864
  73.7 0.9 %copy.16 = f32[4,3,2,64,128]{4,3,2,1,0:T(8,128)} copy(f32[4,3,2,64,128]{4,3,2,1,0:T(8,128)S(1)} %get-tuple-element.5) | data formatting | bytes 1572864
Async XLA Ops:
  1.4 1.1 %copy-start = (f32[4,3,2,64,128]{4,3,2,1,0:T(8,128)S(1)}, f32[4,3,2,64,128]{4,3,2,1,0:T(8,128)}, u32[]{:S(2)}) copy-start(f32[4,3,2,64,128]{4,3,2,1,0:T(8,128)} %args_0_.4) | copy-start | bytes 2359300
  2.5 1.1 %copy-start.1 = (f32[4,3,2,64,128]{4,3,2,1,0:T(8,128)S(1)}, f32[4,3,2,64,128]{4,3,2,1,0:T(8,128)}, u32[]{:S(2)}) copy-start(f32[4,3,2,64,128]{4,3,2,1,0:T(8,128)} %args_1_.4) | copy-start | bytes 2359300
  3.7 1.0 %copy-start.2 = (bf16[4,3,2,64,128]{4,3,2,1,0:T(8,128)(2,1)S(1)}, bf16[4,3,2,64,128]{4,3,2,1,0:T(8,128)(2,1)}, u32[]{:S(2)}) copy-start(bf16[4,3,2,64,128]{4,3,2,1,0:T(8,128)(2,1)} %args_2_.4) | copy-start | bytes 1179652
  4.7 0.7 copy-start.3
  5.3 1.4 %copy-start.4 = (bf16[2,512,768]{2,1,0:T(8,128)(2,1)S(1)}, bf16[2,512,768]{2,1,0:T(8,128)(2,1)}, u32[]{:S(2)}) copy-start(bf16[2,512,768]{2,1,0:T(8,128)(2,1)} %constant.20.args_5_) | copy-start | bytes 4718596
  6.7 0.9 %copy-start.5 = (f32[2,192,64]{2,1,0:T(8,128)S(1)}, f32[2,192,64]{2,1,0:T(8,128)}, u32[]{:S(2)}) copy-start(f32[2,192,64]{2,1,0:T(8,128)} %constant.13.clone.args_8_) | copy-start | bytes 294916
  7.7 0.9 %copy-start.6 = (f32[2,64,192]{2,1,0:T(8,128)S(1)}, f32[2,64,192]{2,1,0:T(8,128)}, u32[]{:S(2)}) copy-start(f32[2,64,192]{2,1,0:T(8,128)} %constant.12.clone.args_7_) | copy-start | bytes 294916
  8.6 0.8 %copy-start.7 = (f32[64,128]{1,0:T(8,128)S(1)}, f32[64,128]{1,0:T(8,128)}, u32[]{:S(2)}) copy-start(f32[64,128]{1,0:T(8,128)} %constant.14.clone.args_9_) | copy-start | bytes 98308

commit v2 on v1

--- a/solution.py
+++ b/solution.py
@@ -78,13 +78,13 @@
 def step_kernel(
     groups,
     slabs,
-    state_ref, adj_ref, obs_ref, spacing_ref, slot_ref, synth_ref, anal_ref, fwd_ref, bwd_ref, w2_ref,
-    next_ref, start_ref,
-    state_v, adj_v, obs_v, synth_v, anal_v, fwd_v, bwd_v, w2_v,
+    state_ref, adj_ref, obs_ref, spacing_h, slot_h, synth_ref, anal_ref, fwd_ref, bwd_ref, w2_ref,
+    next_o, start_o,
+    spacing_ref, slot_ref, state_v, adj_v, obs_v, synth_v, anal_v, fwd_v, bwd_v, w2_v,
     send_v, state_r, forcing_r, next_r, start_r, quad_v, scale_v, mult_v,
     even_v, odd_v, prod_v, modal_v, num_v, psi_v, cot_v, spread_v, pcot_v,
-    edge_send, edge_recv, mass_send, mass_recv, out_v,
-    load_sem, send_sem, recv_sem, esend_sem, erecv_sem, msend_sem, mrecv_sem, out_sem,
+    edge_send, edge_recv, mass_send, mass_recv,
+    load_sem, send_sem, recv_sem, esend_sem, erecv_sem, msend_sem, mrecv_sem,
 ):
     member = lax.axis_index("modes")
     slab = lax.axis_index("elems")
@@ -97,12 +97,15 @@
     loads = [
         pltpu.make_async_copy(src, dst, load_sem.at[i])
         for i, (src, dst) in enumerate(
-            (
-                (state_ref, state_v), (adj_ref, adj_v), (obs_ref, obs_v), (w2_ref, w2_v),
+            [(slot_h, slot_ref), (spacing_h, spacing_ref)]
+            + [(state_ref.at[j], state_v.at[j]) for j in range(ROWS)]
+            + [
+                (adj_ref, adj_v), (obs_ref, obs_v), (w2_ref, w2_v),
                 (fwd_ref, fwd_v), (synth_ref, synth_v), (anal_ref, anal_v), (bwd_ref, bwd_v),
-            )
+            ]
         )
     ]
+    adj_load, obs_load, w2_load, fwd_load, synth_load, anal_load, bwd_load = loads[2 + ROWS :]
     for load in loads:
         load.start()
 
@@ -112,7 +115,12 @@
     for near in (low_slab, high_slab):
         pl.semaphore_signal(barrier, inc=1, device_id={"elems": near}, device_id_type=MESH)
 
+    loads[0].wait()
+    loads[1].wait()
     slots = [slot_ref[0, j] for j in range(ROWS)]
+
+    def rows_of(index, count=NODES):
+        return pl.ds(index * count, count)
 
     def flat(block):
         return block.reshape(6 * NODES, 128)
@@ -123,43 +131,52 @@
             place = jnp.where(slots[j] == row, j, place)
         return place
 
-    def swap(phase, partner):
+    whole = (0, 6 * NODES)
+    phases = ((0,) + whole, (1, 0, 4 * NODES), (1, 4 * NODES, 6 * NODES), (2,) + whole, (3,) + whole)
+
+    def swap(phase, partner, arrival=False):
+        which, begin, end = phases[phase]
+        rows = pl.ds(begin, end - begin)
+        slot = partner if arrival else member
         return pltpu.make_async_remote_copy(
-            src_ref=send_v.at[phase, partner],
-            dst_ref=recv[phase].at[member],
+            src_ref=send_v.at[which, partner, rows],
+            dst_ref=recv[which].at[slot, rows],
             send_sem=send_sem.at[phase, partner],
-            recv_sem=recv_sem.at[phase, member],
+            recv_sem=recv_sem.at[phase, slot],
             device_id={"modes": partner},
             device_id_type=MESH,
         )
 
-    def swapped(phase, partner):
-        return pltpu.make_async_remote_copy(
-            src_ref=send_v.at[phase, partner],
-            dst_ref=recv[phase].at[partner],
-            send_sem=send_sem.at[phase, partner],
-            recv_sem=recv_sem.at[phase, partner],
-            device_id={"modes": partner},
-            device_id_type=MESH,
-        )
-
-    loads[0].wait()
+    def start(phase):
+        for partner in partners:
+            swap(phase, partner).start()
+
+    def sent(phase):
+        for partner in partners:
+            swap(phase, partner).wait_send()
+
+    def arrived(phase):
+        for partner in partners:
+            swap(phase, partner, arrival=True).wait_recv()
+
+    for load in loads[2 : 2 + ROWS]:
+        load.wait()
+    for row in range(ROWS):
+        send_v[0, row] = flat(state_v[elem_of(row)]).astype(LOW)
     pl.semaphore_wait(barrier, 5)
-    for partner in partners:
-        send_v[0, partner] = flat(state_v[elem_of(partner)]).astype(LOW)
-        swap(0, partner).start()
-    state_r[member] = flat(state_v[elem_of(member)]).astype(LOW)
-
-    loads[3].wait()
+    start(0)
+    state_r[member] = send_v[0, member]
+
+    w2_load.wait()
     own = elem_of(member)
     above = elem_of(jnp.minimum(member + 1, ROWS - 1))
     below = elem_of(jnp.maximum(member - 1, 0))
 
     def area(elem):
-        return spacing_ref[elem, 0] * spacing_ref[elem, 1] * 0.25
-
-    side_x = spacing_ref[own, 0]
-    side_y = spacing_ref[own, 1]
+        return spacing_ref[0, elem] * spacing_ref[1, elem] * 0.25
+
+    side_x = spacing_ref[0, own]
+    side_y = spacing_ref[1, own]
     full = (NODES, 128)
     layer = lax.rem(lax.broadcasted_iota(jnp.int32, full, 0), GLL)
     has_above = jnp.logical_and(layer == GLL - 1, member < ROWS - 1)
@@ -189,12 +206,57 @@
     node_a = lax.broadcasted_iota(jnp.int32, full, 0) // GLL
     mult_v[...] = jnp.where(jnp.logical_or(node_a == 0, node_a == GLL - 1), 2.0 * copies, copies)
 
-    loads[1].wait()
-    loads[2].wait()
-    for partner in partners:
-        elem = elem_of(partner)
-        send_v[1, partner] = flat(adj_v[elem] - obs_v[elem].astype(F32)).astype(LOW)
-    forcing_r[member] = flat(adj_v[own] - obs_v[own].astype(F32)).astype(LOW)
+    edge_rows = 6 * GLL * groups
+    top = pl.ds(GLL - 1, edge_rows, stride=GLL)
+    low = pl.ds(0, edge_rows, stride=GLL)
+
+    def edge_copy(which, way):
+        if way == 0:
+            target = {"modes": jnp.minimum(member + 1, ROWS - 1)}
+        elif way == 1:
+            target = {"modes": jnp.maximum(member - 1, 0)}
+        else:
+            target = {"elems": (high_slab, low_slab)[way - 2]}
+        return pltpu.make_async_remote_copy(
+            src_ref=edge_send.at[which, way],
+            dst_ref=edge_recv.at[which, way],
+            send_sem=esend_sem.at[which, way],
+            recv_sem=erecv_sem.at[which, way],
+            device_id=target,
+            device_id_type=MESH,
+        )
+
+    def send_around(which, buf):
+        for way, begin in ((2, NODES - GLL), (3, 0)):
+            edge_send[which, way] = jnp.concatenate(
+                [buf[pl.ds(i * NODES + begin, GLL), :] for i in range(6 * groups)], axis=0
+            ).astype(LOW)
+            edge_copy(which, way).start()
+
+    def add_around(which, buf):
+        for way, begin in ((2, 0), (3, NODES - GLL)):
+            edge_copy(which, way).wait_recv()
+            came = edge_recv[which, way].astype(F32)
+            for i in range(6 * groups):
+                rows = pl.ds(i * NODES + begin, GLL)
+                buf[rows, :] = buf[rows, :] + came[i * GLL : (i + 1) * GLL]
+
+    def around_sent(which):
+        for way in (2, 3):
+            edge_copy(which, way).wait_send()
+
+    adj_load.wait()
+    obs_load.wait()
+    for row in range(ROWS):
+        elem = elem_of(row)
+        psi_v[rows_of(row, 6 * NODES), :] = flat(adj_v[elem] - obs_v[elem].astype(F32))
+    for row in range(ROWS - 1):
+        lower = pl.ds(row * 6 * NODES + GLL - 1, 6 * GLL, stride=GLL)
+        upper = pl.ds((row + 1) * 6 * NODES, 6 * GLL, stride=GLL)
+        both = psi_v[lower, :] + psi_v[upper, :]
+        psi_v[lower, :] = both
+        psi_v[upper, :] = both
+    send_around(0, psi_v)
 
     mass_copy(0).wait()
     mass_copy(1).wait()
@@ -203,8 +265,15 @@
     at_wall = jnp.logical_and(layer == 0, member == 0)
     scale_v[...] = jnp.where(at_wall, 0.0, 1.0) / scale_v[...]
 
-    loads[4].wait()
-    loads[7].wait()
+    add_around(0, psi_v)
+    for row in range(ROWS):
+        send_v[1, row] = psi_v[rows_of(row, 6 * NODES), :].astype(LOW)
+    forcing_r[member] = send_v[1, member]
+    sent(0)
+    start(1)
+
+    fwd_load.wait()
+    bwd_load.wait()
     lane = lax.broadcasted_iota(jnp.int32, (NODES, 3 * NODES), 1)
     ratio = jnp.full((NODES, 3 * NODES), side_y) / jnp.full((NODES, 3 * NODES), side_x)
     coef = jnp.where(
@@ -218,14 +287,7 @@
     )
     bwd_mat = (bwd_v[0] * coef - bwd_v[1] * (viscosity / ratio)).astype(LOW)
 
-    for partner in partners:
-        swap(0, partner).wait_send()
-        swap(1, partner).start()
-    for partner in partners:
-        swapped(0, partner).wait_recv()
-
-    def rows_of(index, count=NODES):
-        return pl.ds(index * count, count)
+    arrived(0)
 
     def gathered(phase, i):
         return jnp.concatenate([recv[phase][q, rows_of(i), :] for q in range(groups)], axis=1)
@@ -243,7 +305,7 @@
     mode_ids = lax.broadcasted_iota(jnp.int32, (NODES, modes), 1)
     wave = mode_ids.astype(F32) * (wave_scale / modes)
 
-    loads[5].wait()
+    synth_load.wait()
     even_v[...] = jnp.dot(
         jnp.concatenate([gathered(0, 2 * c) for c in range(3)], axis=0),
         synth_v[0],
@@ -260,7 +322,7 @@
         er, orr = even_v[rows_of(right), :], odd_v[rows_of(right), :]
         prod_v[0, rows_of(q), :] = (el * er + ol * orr).astype(LOW)
         prod_v[1, rows_of(q), :] = (el * orr + ol * er).astype(LOW)
-    loads[6].wait()
+    anal_load.wait()
     for p in range(2):
         modal_v[p] = jnp.dot(prod_v[p], anal_v[p], preferred_element_type=F32).astype(LOW)
 
@@ -285,91 +347,48 @@
                 + wide(quad_v[...]) * (local + turn * flux_z),
             )
 
-    edge_rows = 6 * GLL * groups
-
-    def assemble(which, buf):
-        def edge_copy(way):
-            if way == 0:
-                target = {"modes": jnp.minimum(member + 1, ROWS - 1)}
-            elif way == 1:
-                target = {"modes": jnp.maximum(member - 1, 0)}
-            else:
-                target = {"elems": (high_slab, low_slab)[way - 2]}
-            return pltpu.make_async_remote_copy(
-                src_ref=edge_send.at[which, way],
-                dst_ref=edge_recv.at[which, way],
-                send_sem=esend_sem.at[which, way],
-                recv_sem=erecv_sem.at[which, way],
-                device_id=target,
-                device_id_type=MESH,
-            )
-
-        top = pl.ds(GLL - 1, edge_rows, stride=GLL)
-        low = pl.ds(0, edge_rows, stride=GLL)
-
-        @pl.when(member < ROWS - 1)
-        def _():
-            edge_send[which, 0] = buf[top, :].astype(LOW)
-            edge_copy(0).start()
-
-        @pl.when(member > 0)
-        def _():
-            edge_send[which, 1] = buf[low, :].astype(LOW)
-            edge_copy(1).start()
-
-        @pl.when(member > 0)
-        def _():
-            edge_copy(0).wait_recv()
-            buf[low, :] = buf[low, :] + edge_recv[which, 0].astype(F32)
-
-        @pl.when(member < ROWS - 1)
-        def _():
-            edge_copy(1).wait_recv()
-            buf[top, :] = buf[top, :] + edge_recv[which, 1].astype(F32)
-
-        for way, start in ((2, NODES - GLL), (3, 0)):
-            edge_send[which, way] = jnp.concatenate(
-                [buf[pl.ds(i * NODES + start, GLL), :] for i in range(6 * groups)], axis=0
-            ).astype(LOW)
-            edge_copy(way).start()
-        for way, start in ((2, 0), (3, NODES - GLL)):
-            edge_copy(way).wait_recv()
-            came = edge_recv[which, way].astype(F32)
-            for i in range(6 * groups):
-                rows = pl.ds(i * NODES + start, GLL)
-                buf[rows, :] = buf[rows, :] + came[i * GLL : (i + 1) * GLL]
-        for way in (2, 3):
-            edge_copy(way).wait_send()
-
-        @pl.when(member < ROWS - 1)
-        def _():
-            edge_copy(0).wait_send()
-
-        @pl.when(member > 0)
-        def _():
-            edge_copy(1).wait_send()
-
-    assemble(0, num_v)
+    send_around(1, num_v)
+    add_around(1, num_v)
+
+    @pl.when(member < ROWS - 1)
+    def _():
+        edge_send[1, 0] = num_v[top, :].astype(LOW)
+        edge_copy(1, 0).start()
+
+    @pl.when(member > 0)
+    def _():
+        edge_send[1, 1] = num_v[low, :].astype(LOW)
+        edge_copy(1, 1).start()
+
+    sent(1)
+    start(2)
+
+    @pl.when(member > 0)
+    def _():
+        edge_copy(1, 0).wait_recv()
+        num_v[low, :] = num_v[low, :] + edge_recv[1, 0].astype(F32)
+
+    @pl.when(member < ROWS - 1)
+    def _():
+        edge_copy(1, 1).wait_recv()
+        num_v[top, :] = num_v[top, :] + edge_recv[1, 1].astype(F32)
+
     for q in range(groups):
         for i in range(6):
             value = scale_v[...] * num_v[rows_of(6 * q + i), :]
             num_v[rows_of(6 * q + i), :] = value
             send_v[2, q, rows_of(i), :] = value.astype(LOW)
-    for partner in partners:
-        swap(1, partner).wait_send()
-        swap(2, partner).start()
     next_r[member] = send_v[2, member]
-
-    for partner in partners:
-        swapped(1, partner).wait_recv()
+    sent(2)
+    start(3)
+
+    arrived(1)
+    arrived(2)
     for q in range(groups):
         for i in range(6):
-            psi_v[rows_of(6 * q + i), :] = scale_v[...] * forcing_r[q, rows_of(i), :].astype(F32)
-    assemble(1, psi_v)
-    for i in range(6 * groups):
-        psi_v[rows_of(i), :] = psi_v[rows_of(i), :] + mult_v[...] * (
-            scale_v[...] * num_v[rows_of(i), :]
-        )
+            rows = rows_of(6 * q + i)
+            forcing = forcing_r[q, rows_of(i), :].astype(F32)
+            psi_v[rows, :] = scale_v[...] * (forcing + mult_v[...] * num_v[rows, :])
 
     norm = jnp.where(mode_ids == 0, 1.0 / (3.0 * modes), 0.5 / (3.0 * modes)).astype(F32)
     for p in range(2):
@@ -412,24 +431,38 @@
             ).astype(LOW)
             for q in range(groups):
                 send_v[3, q, rows_of(2 * c + p), :] = low[:, q * 128 : (q + 1) * 128]
-    for partner in partners:
-        swap(2, partner).wait_send()
-        swap(3, partner).start()
     start_r[member] = send_v[3, member]
-
-    stores = []
-    for which, target in ((0, next_ref), (1, start_ref)):
-        for partner in partners:
-            swapped(2 + which, partner).wait_recv()
+    sent(3)
+    start(4)
+
+    around_sent(0)
+    around_sent(1)
+
+    @pl.when(member < ROWS - 1)
+    def _():
+        edge_copy(1, 0).wait_send()
+
+    @pl.when(member > 0)
+    def _():
+        edge_copy(1, 1).wait_send()
+
+    for phase, rows, target in ((3, next_r, next_o), (4, start_r, start_o)):
+        arrived(phase)
         for j in range(ROWS):
-            out_v[which, j] = recv[2 + which][slots[j]].astype(F32).reshape(3, 2, NODES, 128)
-        store = pltpu.make_async_copy(out_v.at[which], target, out_sem.at[which])
+            target[j] = rows[slots[j]].astype(F32).reshape(3, 2, NODES, 128)
+    sent(4)
+
+
+def store_kernel(next_v, start_v, next_ref, start_ref, sem):
+    stores = [
+        pltpu.make_async_copy(source.at[j], target.at[j], sem.at[which, j])
+        for which, (source, target) in enumerate(((next_v, next_ref), (start_v, start_ref)))
+        for j in range(ROWS)
+    ]
+    for store in stores:
         store.start()
-        stores.append(store)
     for store in stores:
         store.wait()
-    for partner in partners:
-        swap(3, partner).wait_send()
 
 
 def on_device(state, adjoint_end, observed, spacing, radial_slot):
@@ -439,8 +472,8 @@
     half = 3 * modes // 2
     synth, analysis = half_tables(modes, 3 * modes)
     fwd, bwd, w2 = node_tables()
-    any_spec = pl.BlockSpec(memory_space=pl.ANY)
-    smem_spec = pl.BlockSpec(memory_space=pltpu.SMEM)
+    any_spec = pl.BlockSpec(memory_space=pltpu.HBM)
+    vmem_spec = pl.BlockSpec(memory_space=pltpu.VMEM)
     local = state.shape
     block = (6 * NODES, 128)
     vm = pltpu.VMEM
@@ -449,12 +482,18 @@
     def run(*args):
         step_kernel(groups, slabs, *args)
 
-    return pl.pallas_call(
+    held_out = pltpu.VMEM(local, F32)
+
+    def held(array):
+        return pltpu.with_memory_space_constraint(array, pltpu.HBM)
+
+    next_v, start_v = pl.pallas_call(
         run,
-        out_shape=(jax.ShapeDtypeStruct(local, F32), jax.ShapeDtypeStruct(local, F32)),
-        in_specs=[any_spec] * 3 + [smem_spec] * 2 + [any_spec] * 5,
-        out_specs=(any_spec, any_spec),
+        out_shape=(held_out, held_out),
+        in_specs=[any_spec] * 10,
+        out_specs=(vmem_spec, vmem_spec),
         scratch_shapes=[
+            pltpu.SMEM((2, ROWS), F32), pltpu.SMEM((1, ROWS), jnp.int32),
             vm(local, F32), vm(local, F32), vm(local, LOW),
             vm((2, modes, half), LOW), vm((2, half, modes), LOW),
             vm((2, NODES, 3 * NODES), F32), vm((2, 3 * NODES, NODES), F32), vm((NODES, 128), F32),
@@ -467,9 +506,8 @@
             vm((2, 3 * NODES, half), LOW),
             vm((2, 4, 6 * GLL * groups, 128), LOW), vm((2, 4, 6 * GLL * groups, 128), LOW),
             vm((2, GLL, 128), F32), vm((2, GLL, 128), F32),
-            vm((2,) + local, F32),
-            sem((8,)), sem((4, ROWS)), sem((4, ROWS)), sem((2, 4)), sem((2, 4)),
-            sem((2,)), sem((2,)), sem((2,)),
+            sem((9 + ROWS,)), sem((5, ROWS)), sem((5, ROWS)), sem((2, 4)), sem((2, 4)),
+            sem((2,)), sem((2,)),
         ],
         compiler_params=pltpu.CompilerParams(
             collective_id=0, has_side_effects=True, vmem_limit_bytes=48 * 1024 * 1024
@@ -478,11 +516,19 @@
             flops=1900000000, bytes_accessed=7000000, transcendentals=0
         ),
     )(
-        state, adjoint_end, observed, spacing, radial_slot,
-        jnp.asarray(synth, F32).astype(LOW), jnp.asarray(analysis, F32).astype(LOW),
-        jnp.asarray(fwd, F32), jnp.asarray(bwd, F32),
-        jnp.asarray(np.broadcast_to(w2[:, None], (NODES, 128)), F32),
-    )
+        held(state), held(adjoint_end), held(observed), held(spacing.T), held(radial_slot),
+        held(jnp.asarray(synth, F32).astype(LOW)), held(jnp.asarray(analysis, F32).astype(LOW)),
+        held(jnp.asarray(fwd, F32)), held(jnp.asarray(bwd, F32)),
+        held(jnp.asarray(np.broadcast_to(w2[:, None], (NODES, 128)), F32)),
+    )
+    return pl.pallas_call(
+        store_kernel,
+        out_shape=(jax.ShapeDtypeStruct(local, F32), jax.ShapeDtypeStruct(local, F32)),
+        in_specs=[pl.BlockSpec(memory_space=pl.ANY)] * 2,
+        out_specs=(any_spec, any_spec),
+        scratch_shapes=[sem((2, ROWS))],
+        compiler_params=pltpu.CompilerParams(vmem_limit_bytes=1024 * 1024),
+    )(next_v, start_v)
 
 
 def solution(mesh):

time: 75 us -> 57 us (0.76)
  local copies, waits for them, and re-layouts: 10.4 us -> 0 us
  Pallas kernels: 63.5 us -> 56.3 us
    unnamed x19 -> x0, local copies, waits for them, and re-layouts: 10.4 us -> none
    pallas_call x1 -> x2, Pallas kernels: 63.5 us -> 56.3 us  [the longest x1 55.1 us: on_device(): pl.pallas_call(run, out_shape=(held_out, held_out), in_specs=[any_spec] *...]
where the time goes in v2:
time: 57 us; the launch traced here: 56.9 us
  Pallas kernels  56.3 us (99%)
  between operations  0.64 us (1%)
    pallas_call x1, Pallas kernels, on_device(): pl.pallas_call(run, out_shape=(held_out, held_out), in_specs=[any_spec] *...  55.1 us
    pallas_call x1, Pallas kernels, on_device(): pl.pallas_call(store_kernel, out_shape=(jax.ShapeDtypeStruct(local, F32),...  1.2 us

profile of v2, /device:TPU:8, one launch (start us, length us, event | category | flops | bytes accessed | tf_op | source)
XLA Modules:
  0.0 56.9 jit_solution(10704131590120942504)
XLA Ops:
  0.6 55.1 %shard_map.113 = (f32[4,3,2,64,128]{4,3,2,1,0:T(8,128)S(1)}, f32[4,3,2,64,128]{4,3,2,1,0:T(8,128)S(1)}) custom-call(f32[4,3,2,64,128]{4,3,2,1,0:T(8,128)} %args_0_.4, f32[4,3,2,64,128]{4,3,2,1,0:T(8,128)} %args_1_.4, bf16[4,3,2,64,128]{4,3,2,1,0:T(8,128)(2,1)} %args_2_.4, f32[2,4]{1,0:T(2,128)} %bitcast.1, s32[1,4]{1,0:T(1,128)} %args_4_.4, ...), custom_call_target="tpu_custom_call" | custom-call | flops 1900000000 | bytes 7000000 | tf_op jit(solution)/shard_map/pallas_call | solution.py:490
  55.7 1.2 %shard_map.114 = (f32[4,3,2,64,128]{4,3,2,1,0:T(8,128)}, f32[4,3,2,64,128]{4,3,2,1,0:T(8,128)}) custom-call(f32[4,3,2,64,128]{4,3,2,1,0:T(8,128)S(1)} %get-tuple-element.4.next_v, f32[4,3,2,64,128]{4,3,2,1,0:T(8,128)S(1)} %get-tuple-element.5.start_v), custom_call_target="tpu_custom_call" | custom-call | tf_op jit(solution)/shard_map/pallas_call | solution.py:524

commit v3 on v2

--- a/solution.py
+++ b/solution.py
@@ -112,8 +112,20 @@
     barrier = pltpu.get_barrier_semaphore()
     for partner in partners:
         pl.semaphore_signal(barrier, inc=1, device_id={"modes": partner}, device_id_type=MESH)
-    for near in (low_slab, high_slab):
+
+    def greet(near):
         pl.semaphore_signal(barrier, inc=1, device_id={"elems": near}, device_id_type=MESH)
+
+    first = slab == 0
+    last = slab == slabs - 1
+
+    @pl.when(jnp.logical_not(first))
+    def _():
+        greet(low_slab)
+
+    @pl.when(jnp.logical_not(last))
+    def _():
+        greet(high_slab)
 
     loads[0].wait()
     loads[1].wait()
@@ -132,7 +144,27 @@
         return place
 
     whole = (0, 6 * NODES)
-    phases = ((0,) + whole, (1, 0, 4 * NODES), (1, 4 * NODES, 6 * NODES), (2,) + whole, (3,) + whole)
+    inner = NODES - 2 * GLL
+    edges = 6 * inner
+    phases = (
+        (0,) + whole,
+        (1, 0, 4 * inner), (1, 4 * inner, edges), (1, edges, 6 * NODES),
+        (2, 0, edges), (2, edges, 6 * NODES),
+        (3,) + whole,
+    )
+
+    def pack_inner(which, slot, i, value):
+        send_v[which, slot, pl.ds(i * inner, inner), :] = value.astype(LOW)
+
+    def pack_edges(which, slot, i, low_edge, high_edge):
+        send_v[which, slot, pl.ds(edges + i * 2 * GLL, 2 * GLL), :] = jnp.concatenate(
+            [low_edge, high_edge], axis=0
+        ).astype(LOW)
+
+    def unpack(block, i):
+        sides = block[edges + i * 2 * GLL : edges + (i + 1) * 2 * GLL]
+        middle = block[i * inner : (i + 1) * inner]
+        return jnp.concatenate([sides[:GLL], middle, sides[GLL:]], axis=0)
 
     def swap(phase, partner, arrival=False):
         which, begin, end = phases[phase]
@@ -163,7 +195,20 @@
         load.wait()
     for row in range(ROWS):
         send_v[0, row] = flat(state_v[elem_of(row)]).astype(LOW)
-    pl.semaphore_wait(barrier, 5)
+
+    @pl.when(first)
+    def _():
+        pl.semaphore_wait(barrier, 4)
+        greet(low_slab)
+
+    @pl.when(jnp.logical_not(first))
+    def _():
+        pl.semaphore_wait(barrier, 5)
+
+    @pl.when(last)
+    def _():
+        greet(high_slab)
+
     start(0)
     state_r[member] = send_v[0, member]
 
@@ -186,7 +231,9 @@
     quad_v[...] = quad
     mass = quad + jnp.where(has_above, w2 * area(above), 0.0)
     mass = mass + jnp.where(has_below, w2 * area(below), 0.0)
-    scale_v[...] = mass
+    at_wall = jnp.logical_and(layer == 0, member == 0)
+    keep = jnp.where(at_wall, 0.0, 1.0)
+    scale_v[...] = keep / mass
     mass_send[0] = mass[NODES - GLL :]
     mass_send[1] = mass[:GLL]
 
@@ -200,8 +247,6 @@
             device_id_type=MESH,
         )
 
-    mass_copy(0).start()
-    mass_copy(1).start()
     copies = jnp.where(jnp.logical_or(has_above, has_below), 2.0, 1.0).astype(F32)
     node_a = lax.broadcasted_iota(jnp.int32, full, 0) // GLL
     mult_v[...] = jnp.where(jnp.logical_or(node_a == 0, node_a == GLL - 1), 2.0 * copies, copies)
@@ -226,12 +271,11 @@
             device_id_type=MESH,
         )
 
-    def send_around(which, buf):
+    def pack_around(which, buf):
         for way, begin in ((2, NODES - GLL), (3, 0)):
             edge_send[which, way] = jnp.concatenate(
                 [buf[pl.ds(i * NODES + begin, GLL), :] for i in range(6 * groups)], axis=0
             ).astype(LOW)
-            edge_copy(which, way).start()
 
     def add_around(which, buf):
         for way, begin in ((2, 0), (3, NODES - GLL)):
@@ -256,19 +300,23 @@
         both = psi_v[lower, :] + psi_v[upper, :]
         psi_v[lower, :] = both
         psi_v[upper, :] = both
-    send_around(0, psi_v)
-
-    mass_copy(0).wait()
-    mass_copy(1).wait()
-    scale_v[:GLL, :] = scale_v[:GLL, :] + mass_recv[0]
-    scale_v[NODES - GLL :, :] = scale_v[NODES - GLL :, :] + mass_recv[1]
-    at_wall = jnp.logical_and(layer == 0, member == 0)
-    scale_v[...] = jnp.where(at_wall, 0.0, 1.0) / scale_v[...]
-
-    add_around(0, psi_v)
+    pack_around(0, psi_v)
+    mass_copy(0).start()
+    edge_copy(0, 2).start()
+
+    def send_back():
+        mass_copy(1).start()
+        edge_copy(0, 3).start()
+
+    @pl.when(jnp.logical_not(first))
+    def _():
+        send_back()
+
     for row in range(ROWS):
-        send_v[1, row] = psi_v[rows_of(row, 6 * NODES), :].astype(LOW)
-    forcing_r[member] = send_v[1, member]
+        for i in range(6):
+            rows = pl.ds((6 * row + i) * NODES + GLL, inner)
+            pack_inner(1, row, i, psi_v[rows, :])
+    forcing_r[member, pl.ds(0, edges), :] = send_v[1, member, pl.ds(0, edges), :]
     sent(0)
     start(1)
 
@@ -347,9 +395,6 @@
                 + wide(quad_v[...]) * (local + turn * flux_z),
             )
 
-    send_around(1, num_v)
-    add_around(1, num_v)
-
     @pl.when(member < ROWS - 1)
     def _():
         edge_send[1, 0] = num_v[top, :].astype(LOW)
@@ -360,8 +405,26 @@
         edge_send[1, 1] = num_v[low, :].astype(LOW)
         edge_copy(1, 1).start()
 
-    sent(1)
     start(2)
+
+    @pl.when(first)
+    def _():
+        pl.semaphore_wait(barrier, 1)
+        send_back()
+
+    mass_copy(0).wait()
+    mass_copy(1).wait()
+    scale_v[:GLL, :] = keep[:GLL] / (mass_send[1] + mass_recv[0])
+    scale_v[NODES - GLL :, :] = keep[NODES - GLL :] / (mass_send[0] + mass_recv[1])
+    add_around(0, psi_v)
+    for row in range(ROWS):
+        for i in range(6):
+            base = (6 * row + i) * NODES
+            pack_edges(
+                1, row, i, psi_v[pl.ds(base, GLL), :], psi_v[pl.ds(base + NODES - GLL, GLL), :]
+            )
+    forcing_r[member, pl.ds(edges, 12 * GLL), :] = send_v[1, member, pl.ds(edges, 12 * GLL), :]
+    start(3)
 
     @pl.when(member > 0)
     def _():
@@ -373,22 +436,40 @@
         edge_copy(1, 1).wait_recv()
         num_v[top, :] = num_v[top, :] + edge_recv[1, 1].astype(F32)
 
+    pack_around(1, num_v)
+    edge_copy(1, 2).start()
+    edge_copy(1, 3).start()
     for q in range(groups):
         for i in range(6):
-            value = scale_v[...] * num_v[rows_of(6 * q + i), :]
-            num_v[rows_of(6 * q + i), :] = value
-            send_v[2, q, rows_of(i), :] = value.astype(LOW)
-    next_r[member] = send_v[2, member]
+            rows = pl.ds((6 * q + i) * NODES + GLL, inner)
+            value = scale_v[GLL : NODES - GLL, :] * num_v[rows, :]
+            num_v[rows, :] = value
+            pack_inner(2, q, i, value)
+    next_r[member, pl.ds(0, edges), :] = send_v[2, member, pl.ds(0, edges), :]
+    sent(1)
     sent(2)
-    start(3)
+    sent(3)
+    start(4)
+    add_around(1, num_v)
+    for q in range(groups):
+        for i in range(6):
+            base = (6 * q + i) * NODES
+            low_edge = scale_v[:GLL, :] * num_v[pl.ds(base, GLL), :]
+            num_v[pl.ds(base, GLL), :] = low_edge
+            high_edge = scale_v[NODES - GLL :, :] * num_v[pl.ds(base + NODES - GLL, GLL), :]
+            num_v[pl.ds(base + NODES - GLL, GLL), :] = high_edge
+            pack_edges(2, q, i, low_edge, high_edge)
+    next_r[member, pl.ds(edges, 12 * GLL), :] = send_v[2, member, pl.ds(edges, 12 * GLL), :]
+    start(5)
 
     arrived(1)
     arrived(2)
+    arrived(3)
     for q in range(groups):
+        block = forcing_r[q].astype(F32)
         for i in range(6):
             rows = rows_of(6 * q + i)
-            forcing = forcing_r[q, rows_of(i), :].astype(F32)
-            psi_v[rows, :] = scale_v[...] * (forcing + mult_v[...] * num_v[rows, :])
+            psi_v[rows, :] = scale_v[...] * (unpack(block, i) + mult_v[...] * num_v[rows, :])
 
     norm = jnp.where(mode_ids == 0, 1.0 / (3.0 * modes), 0.5 / (3.0 * modes)).astype(F32)
     for p in range(2):
@@ -432,8 +513,9 @@
             for q in range(groups):
                 send_v[3, q, rows_of(2 * c + p), :] = low[:, q * 128 : (q + 1) * 128]
     start_r[member] = send_v[3, member]
-    sent(3)
-    start(4)
+    sent(4)
+    sent(5)
+    start(6)
 
     around_sent(0)
     around_sent(1)
@@ -446,11 +528,16 @@
     def _():
         edge_copy(1, 1).wait_send()
 
-    for phase, rows, target in ((3, next_r, next_o), (4, start_r, start_o)):
-        arrived(phase)
-        for j in range(ROWS):
-            target[j] = rows[slots[j]].astype(F32).reshape(3, 2, NODES, 128)
-    sent(4)
+    arrived(4)
+    arrived(5)
+    for j in range(ROWS):
+        block = next_r[slots[j]].astype(F32)
+        for i in range(6):
+            next_o[j, i // 2, i % 2] = unpack(block, i)
+    arrived(6)
+    for j in range(ROWS):
+        start_o[j] = start_r[slots[j]].astype(F32).reshape(3, 2, NODES, 128)
+    sent(6)
 
 
 def store_kernel(next_v, start_v, next_ref, start_ref, sem):
@@ -506,7 +593,7 @@
             vm((2, 3 * NODES, half), LOW),
             vm((2, 4, 6 * GLL * groups, 128), LOW), vm((2, 4, 6 * GLL * groups, 128), LOW),
             vm((2, GLL, 128), F32), vm((2, GLL, 128), F32),
-            sem((9 + ROWS,)), sem((5, ROWS)), sem((5, ROWS)), sem((2, 4)), sem((2, 4)),
+            sem((9 + ROWS,)), sem((7, ROWS)), sem((7, ROWS)), sem((2, 4)), sem((2, 4)),
             sem((2,)), sem((2,)),
         ],
         compiler_params=pltpu.CompilerParams(

time: 57 us -> 49.1 us (0.86)
  the two profiles are of different devices: /device:TPU:8 before, /device:TPU:16 now
where the time goes in v3:
time: 49.1 us; the launch traced here: 49 us
  Pallas kernels  48.3 us (98%)
  between operations  0.64 us (1%)
    pallas_call x1, Pallas kernels, on_device(): pl.pallas_call(run, out_shape=(held_out, held_out), in_specs=[any_spec] *...  47.1 us
    pallas_call x1, Pallas kernels, on_device(): pl.pallas_call(store_kernel, out_shape=(jax.ShapeDtypeStruct(local, F32),...  1.2 us

profile of v3, /device:TPU:16, one launch (start us, length us, event | category | flops | bytes accessed | tf_op | source)
XLA Modules:
  0.0 49.0 jit_solution(1162837068092319676)
XLA Ops:
  0.6 47.1 %shard_map.113 = (f32[4,3,2,64,128]{4,3,2,1,0:T(8,128)S(1)}, f32[4,3,2,64,128]{4,3,2,1,0:T(8,128)S(1)}) custom-call(f32[4,3,2,64,128]{4,3,2,1,0:T(8,128)} %args_0_.4, f32[4,3,2,64,128]{4,3,2,1,0:T(8,128)} %args_1_.4, bf16[4,3,2,64,128]{4,3,2,1,0:T(8,128)(2,1)} %args_2_.4, f32[2,4]{1,0:T(2,128)} %bitcast.1, s32[1,4]{1,0:T(1,128)} %args_4_.4, ...), custom_call_target="tpu_custom_call" | custom-call | flops 1900000000 | bytes 7000000 | tf_op jit(solution)/shard_map/pallas_call | solution.py:577
  47.8 1.2 %shard_map.114 = (f32[4,3,2,64,128]{4,3,2,1,0:T(8,128)}, f32[4,3,2,64,128]{4,3,2,1,0:T(8,128)}) custom-call(f32[4,3,2,64,128]{4,3,2,1,0:T(8,128)S(1)} %get-tuple-element.4.next_v, f32[4,3,2,64,128]{4,3,2,1,0:T(8,128)S(1)} %get-tuple-element.5.start_v), custom_call_target="tpu_custom_call" | custom-call | tf_op jit(solution)/shard_map/pallas_call | solution.py:611

commit v4 on v3

--- a/solution.py
+++ b/solution.py
@@ -9,6 +9,7 @@
 GLL = 8
 NODES = GLL * GLL
 ROWS = 4
+CHIP_ROW = 8
 time_step = 0.01
 viscosity = 0.05
 wave_scale = 4.0
@@ -83,7 +84,7 @@
     spacing_ref, slot_ref, state_v, adj_v, obs_v, synth_v, anal_v, fwd_v, bwd_v, w2_v,
     send_v, state_r, forcing_r, next_r, start_r, quad_v, scale_v, mult_v,
     even_v, odd_v, prod_v, modal_v, num_v, psi_v, cot_v, spread_v, pcot_v,
-    edge_send, edge_recv, mass_send, mass_recv,
+    edge_send, edge_recv, stage_v, full_v, mass_send, mass_recv,
     load_sem, send_sem, recv_sem, esend_sem, erecv_sem, msend_sem, mrecv_sem,
 ):
     member = lax.axis_index("modes")
@@ -113,19 +114,39 @@
     for partner in partners:
         pl.semaphore_signal(barrier, inc=1, device_id={"modes": partner}, device_id_type=MESH)
 
-    def greet(near):
-        pl.semaphore_signal(barrier, inc=1, device_id={"elems": near}, device_id_type=MESH)
-
-    first = slab == 0
-    last = slab == slabs - 1
-
-    @pl.when(jnp.logical_not(first))
-    def _():
-        greet(low_slab)
-
-    @pl.when(jnp.logical_not(last))
-    def _():
-        greet(high_slab)
+    place = lax.rem(slab, 2 * CHIP_ROW)
+    early_low = place == 0
+    early_high = place == CHIP_ROW - 1
+    across_low = jnp.logical_or(early_low, place == CHIP_ROW)
+    across_high = jnp.logical_or(early_high, place == 2 * CHIP_ROW - 1)
+    early = jnp.logical_or(early_low, early_high)
+    greet_low_now = jnp.logical_not(across_low)
+    greet_high_now = jnp.logical_not(across_high)
+
+    mirrored = place >= CHIP_ROW
+
+    def flip(index):
+        return jnp.where(mirrored, ROWS - 1 - index, index)
+
+    row_here = flip(member)
+
+    def around(way):
+        across = (across_high, across_low)[way]
+        return {
+            "modes": jnp.where(across, ROWS - 1 - member, member),
+            "elems": (high_slab, low_slab)[way],
+        }
+
+    def greet(way):
+        pl.semaphore_signal(barrier, inc=1, device_id=around(way), device_id_type=MESH)
+
+    @pl.when(greet_low_now)
+    def _():
+        greet(1)
+
+    @pl.when(greet_high_now)
+    def _():
+        greet(0)
 
     loads[0].wait()
     loads[1].wait()
@@ -145,25 +166,20 @@
 
     whole = (0, 6 * NODES)
     inner = NODES - 2 * GLL
-    edges = 6 * inner
+    edges = 12 * GLL
+    spare = 4
+    kept = 6 * inner - spare * GLL
     phases = (
         (0,) + whole,
-        (1, 0, 4 * inner), (1, 4 * inner, edges), (1, edges, 6 * NODES),
-        (2, 0, edges), (2, edges, 6 * NODES),
+        (1, 0, edges + inner), (1, edges + inner, 6 * NODES),
+        (2, 0, kept), (2, kept, kept + 6 * GLL),
         (3,) + whole,
-    )
-
-    def pack_inner(which, slot, i, value):
-        send_v[which, slot, pl.ds(i * inner, inner), :] = value.astype(LOW)
-
-    def pack_edges(which, slot, i, low_edge, high_edge):
-        send_v[which, slot, pl.ds(edges + i * 2 * GLL, 2 * GLL), :] = jnp.concatenate(
-            [low_edge, high_edge], axis=0
-        ).astype(LOW)
+        (2, kept + 6 * GLL, kept + 12 * GLL),
+    )
 
     def unpack(block, i):
-        sides = block[edges + i * 2 * GLL : edges + (i + 1) * 2 * GLL]
-        middle = block[i * inner : (i + 1) * inner]
+        sides = block[i * 2 * GLL : (i + 1) * 2 * GLL]
+        middle = block[edges + i * inner : edges + (i + 1) * inner]
         return jnp.concatenate([sides[:GLL], middle, sides[GLL:]], axis=0)
 
     def swap(phase, partner, arrival=False):
@@ -193,29 +209,34 @@
 
     for load in loads[2 : 2 + ROWS]:
         load.wait()
-    for row in range(ROWS):
-        send_v[0, row] = flat(state_v[elem_of(row)]).astype(LOW)
-
-    @pl.when(first)
+    for device in range(ROWS):
+        send_v[0, device] = flat(state_v[elem_of(flip(device))]).astype(LOW)
+
+    @pl.when(early)
     def _():
         pl.semaphore_wait(barrier, 4)
-        greet(low_slab)
-
-    @pl.when(jnp.logical_not(first))
+
+    @pl.when(jnp.logical_not(early))
     def _():
         pl.semaphore_wait(barrier, 5)
 
-    @pl.when(last)
-    def _():
-        greet(high_slab)
+    @pl.when(jnp.logical_not(greet_low_now))
+    def _():
+        greet(1)
+
+    @pl.when(jnp.logical_not(greet_high_now))
+    def _():
+        greet(0)
 
     start(0)
     state_r[member] = send_v[0, member]
 
     w2_load.wait()
-    own = elem_of(member)
-    above = elem_of(jnp.minimum(member + 1, ROWS - 1))
-    below = elem_of(jnp.maximum(member - 1, 0))
+    own = elem_of(row_here)
+    row_above = jnp.minimum(row_here + 1, ROWS - 1)
+    row_below = jnp.maximum(row_here - 1, 0)
+    above = elem_of(row_above)
+    below = elem_of(row_below)
 
     def area(elem):
         return spacing_ref[0, elem] * spacing_ref[1, elem] * 0.25
@@ -224,14 +245,14 @@
     side_y = spacing_ref[1, own]
     full = (NODES, 128)
     layer = lax.rem(lax.broadcasted_iota(jnp.int32, full, 0), GLL)
-    has_above = jnp.logical_and(layer == GLL - 1, member < ROWS - 1)
-    has_below = jnp.logical_and(layer == 0, member > 0)
+    has_above = jnp.logical_and(layer == GLL - 1, row_here < ROWS - 1)
+    has_below = jnp.logical_and(layer == 0, row_here > 0)
     w2 = w2_v[...]
     quad = w2 * area(own)
     quad_v[...] = quad
     mass = quad + jnp.where(has_above, w2 * area(above), 0.0)
     mass = mass + jnp.where(has_below, w2 * area(below), 0.0)
-    at_wall = jnp.logical_and(layer == 0, member == 0)
+    at_wall = jnp.logical_and(layer == 0, row_here == 0)
     keep = jnp.where(at_wall, 0.0, 1.0)
     scale_v[...] = keep / mass
     mass_send[0] = mass[NODES - GLL :]
@@ -243,7 +264,7 @@
             dst_ref=mass_recv.at[way],
             send_sem=msend_sem.at[way],
             recv_sem=mrecv_sem.at[way],
-            device_id={"elems": (high_slab, low_slab)[way]},
+            device_id=around(way),
             device_id_type=MESH,
         )
 
@@ -257,11 +278,11 @@
 
     def edge_copy(which, way):
         if way == 0:
-            target = {"modes": jnp.minimum(member + 1, ROWS - 1)}
+            target = {"modes": flip(row_above)}
         elif way == 1:
-            target = {"modes": jnp.maximum(member - 1, 0)}
+            target = {"modes": flip(row_below)}
         else:
-            target = {"elems": (high_slab, low_slab)[way - 2]}
+            target = around(way - 2)
         return pltpu.make_async_remote_copy(
             src_ref=edge_send.at[which, way],
             dst_ref=edge_recv.at[which, way],
@@ -300,23 +321,17 @@
         both = psi_v[lower, :] + psi_v[upper, :]
         psi_v[lower, :] = both
         psi_v[upper, :] = both
-    pack_around(0, psi_v)
-    mass_copy(0).start()
-    edge_copy(0, 2).start()
-
-    def send_back():
-        mass_copy(1).start()
-        edge_copy(0, 3).start()
-
-    @pl.when(jnp.logical_not(first))
-    def _():
-        send_back()
-
     for row in range(ROWS):
+        device = flip(row)
         for i in range(6):
-            rows = pl.ds((6 * row + i) * NODES + GLL, inner)
-            pack_inner(1, row, i, psi_v[rows, :])
-    forcing_r[member, pl.ds(0, edges), :] = send_v[1, member, pl.ds(0, edges), :]
+            base = (6 * row + i) * NODES
+            send_v[1, device, pl.ds(i * 2 * GLL, 2 * GLL), :] = jnp.concatenate(
+                [psi_v[pl.ds(base, GLL), :], psi_v[pl.ds(base + NODES - GLL, GLL), :]], axis=0
+            ).astype(LOW)
+            send_v[1, device, pl.ds(edges + i * inner, inner), :] = psi_v[
+                pl.ds(base + GLL, inner), :
+            ].astype(LOW)
+    forcing_r[member] = send_v[1, member]
     sent(0)
     start(1)
 
@@ -395,43 +410,40 @@
                 + wide(quad_v[...]) * (local + turn * flux_z),
             )
 
-    @pl.when(member < ROWS - 1)
+    @pl.when(row_here < ROWS - 1)
     def _():
         edge_send[1, 0] = num_v[top, :].astype(LOW)
         edge_copy(1, 0).start()
 
-    @pl.when(member > 0)
+    @pl.when(row_here > 0)
     def _():
         edge_send[1, 1] = num_v[low, :].astype(LOW)
         edge_copy(1, 1).start()
 
     start(2)
 
-    @pl.when(first)
+    @pl.when(early)
     def _():
         pl.semaphore_wait(barrier, 1)
-        send_back()
-
-    mass_copy(0).wait()
-    mass_copy(1).wait()
-    scale_v[:GLL, :] = keep[:GLL] / (mass_send[1] + mass_recv[0])
-    scale_v[NODES - GLL :, :] = keep[NODES - GLL :] / (mass_send[0] + mass_recv[1])
-    add_around(0, psi_v)
-    for row in range(ROWS):
-        for i in range(6):
-            base = (6 * row + i) * NODES
-            pack_edges(
-                1, row, i, psi_v[pl.ds(base, GLL), :], psi_v[pl.ds(base + NODES - GLL, GLL), :]
-            )
-    forcing_r[member, pl.ds(edges, 12 * GLL), :] = send_v[1, member, pl.ds(edges, 12 * GLL), :]
-    start(3)
-
-    @pl.when(member > 0)
+
+    mass_copy(0).start()
+    mass_copy(1).start()
+    arrived(1)
+    for q in range(groups):
+        block = forcing_r[q, pl.ds(0, edges), :].astype(F32)
+        for way, begin in ((2, GLL), (3, 0)):
+            edge_send[0, way, pl.ds(q * 6 * GLL, 6 * GLL), :] = jnp.concatenate(
+                [block[i * 2 * GLL + begin : i * 2 * GLL + begin + GLL] for i in range(6)], axis=0
+            ).astype(LOW)
+    edge_copy(0, 2).start()
+    edge_copy(0, 3).start()
+
+    @pl.when(row_here > 0)
     def _():
         edge_copy(1, 0).wait_recv()
         num_v[low, :] = num_v[low, :] + edge_recv[1, 0].astype(F32)
 
-    @pl.when(member < ROWS - 1)
+    @pl.when(row_here < ROWS - 1)
     def _():
         edge_copy(1, 1).wait_recv()
         num_v[top, :] = num_v[top, :] + edge_recv[1, 1].astype(F32)
@@ -444,12 +456,22 @@
             rows = pl.ds((6 * q + i) * NODES + GLL, inner)
             value = scale_v[GLL : NODES - GLL, :] * num_v[rows, :]
             num_v[rows, :] = value
-            pack_inner(2, q, i, value)
-    next_r[member, pl.ds(0, edges), :] = send_v[2, member, pl.ds(0, edges), :]
+            if i < 5:
+                stage_v[q, pl.ds(i * inner, inner), :] = value
+            else:
+                stage_v[q, pl.ds(i * inner, inner - spare * GLL), :] = value[: inner - spare * GLL]
+                for k in range(spare):
+                    tile = value[inner - (spare - k) * GLL : inner - (spare - k - 1) * GLL]
+                    stage_v[q, pl.ds(k * GLL * GLL, GLL, stride=GLL), :] = tile
+        send_v[2, q, pl.ds(0, kept), :] = stage_v[q].astype(LOW)
+    next_r[member, pl.ds(0, kept), :] = send_v[2, member, pl.ds(0, kept), :]
     sent(1)
     sent(2)
-    sent(3)
-    start(4)
+    start(3)
+    mass_copy(0).wait()
+    mass_copy(1).wait()
+    scale_v[:GLL, :] = keep[:GLL] / (mass_send[1] + mass_recv[0])
+    scale_v[NODES - GLL :, :] = keep[NODES - GLL :] / (mass_send[0] + mass_recv[1])
     add_around(1, num_v)
     for q in range(groups):
         for i in range(6):
@@ -458,18 +480,26 @@
             num_v[pl.ds(base, GLL), :] = low_edge
             high_edge = scale_v[NODES - GLL :, :] * num_v[pl.ds(base + NODES - GLL, GLL), :]
             num_v[pl.ds(base + NODES - GLL, GLL), :] = high_edge
-            pack_edges(2, q, i, low_edge, high_edge)
-    next_r[member, pl.ds(edges, 12 * GLL), :] = send_v[2, member, pl.ds(edges, 12 * GLL), :]
-    start(5)
-
-    arrived(1)
+            stage_v[q, pl.ds(i * GLL, GLL), :] = low_edge
+            stage_v[q, pl.ds((6 + i) * GLL, GLL), :] = high_edge
+        send_v[2, q, pl.ds(kept, 12 * GLL), :] = stage_v[q, pl.ds(0, 12 * GLL), :].astype(LOW)
+    next_r[member, pl.ds(kept, 12 * GLL), :] = send_v[2, member, pl.ds(kept, 12 * GLL), :]
+    start(4)
+
+    @pl.when(across_high)
+    def _():
+        start(6)
+
     arrived(2)
-    arrived(3)
     for q in range(groups):
         block = forcing_r[q].astype(F32)
         for i in range(6):
             rows = rows_of(6 * q + i)
-            psi_v[rows, :] = scale_v[...] * (unpack(block, i) + mult_v[...] * num_v[rows, :])
+            psi_v[rows, :] = unpack(block, i)
+    add_around(0, psi_v)
+    for i in range(6 * groups):
+        rows = rows_of(i)
+        psi_v[rows, :] = scale_v[...] * (psi_v[rows, :] + mult_v[...] * num_v[rows, :])
 
     norm = jnp.where(mode_ids == 0, 1.0 / (3.0 * modes), 0.5 / (3.0 * modes)).astype(F32)
     for p in range(2):
@@ -513,31 +543,87 @@
             for q in range(groups):
                 send_v[3, q, rows_of(2 * c + p), :] = low[:, q * 128 : (q + 1) * 128]
     start_r[member] = send_v[3, member]
+    sent(3)
     sent(4)
-    sent(5)
-    start(6)
+
+    @pl.when(across_high)
+    def _():
+        sent(6)
+
+    start(5)
 
     around_sent(0)
     around_sent(1)
 
-    @pl.when(member < ROWS - 1)
+    @pl.when(row_here < ROWS - 1)
     def _():
         edge_copy(1, 0).wait_send()
 
-    @pl.when(member > 0)
+    @pl.when(row_here > 0)
     def _():
         edge_copy(1, 1).wait_send()
 
+    arrived(3)
     arrived(4)
+    for row in range(ROWS):
+        edge_send[0, 0, pl.ds(row * 6 * GLL, 6 * GLL), :] = next_r[
+            flip(row), pl.ds(kept, 6 * GLL), :
+        ]
+    side_copy = pltpu.make_async_remote_copy(
+        src_ref=edge_send.at[0, 0],
+        dst_ref=edge_recv.at[0, 0],
+        send_sem=esend_sem.at[0, 0],
+        recv_sem=erecv_sem.at[0, 0],
+        device_id={"elems": low_slab},
+        device_id_type=MESH,
+    )
+
+    @pl.when(jnp.logical_not(across_low))
+    def _():
+        side_copy.start()
+
+    for row in range(ROWS):
+        block = next_r[flip(row), pl.ds(0, kept + 6 * GLL), :].astype(F32)
+        stage_v[row] = block[:kept]
+        for i in range(6):
+            full_v[row, pl.ds(i * NODES, GLL), :] = block[kept + i * GLL : kept + (i + 1) * GLL]
+            count = inner if i < 5 else inner - spare * GLL
+            full_v[row, pl.ds(i * NODES + GLL, count), :] = block[i * inner : i * inner + count]
+        for k in range(spare):
+            tile = stage_v[row, pl.ds(k * GLL * GLL, GLL, stride=GLL), :]
+            full_v[row, pl.ds(6 * NODES - (spare - k + 1) * GLL, GLL), :] = tile
+
+    @pl.when(jnp.logical_not(across_low))
+    def _():
+        side_copy.wait_send()
+
+    @pl.when(jnp.logical_not(across_high))
+    def _():
+        side_copy.wait_recv()
+
+    @pl.when(across_high)
+    def _():
+        arrived(6)
+        for row in range(ROWS):
+            edge_recv[0, 0, pl.ds(row * 6 * GLL, 6 * GLL), :] = next_r[
+                flip(row), pl.ds(kept + 6 * GLL, 6 * GLL), :
+            ]
+
+    for row in range(ROWS):
+        side = edge_recv[0, 0, pl.ds(row * 6 * GLL, 6 * GLL), :].astype(F32)
+        for i in range(6):
+            full_v[row, pl.ds((i + 1) * NODES - GLL, GLL), :] = side[i * GLL : (i + 1) * GLL]
+        if row == 0:
+            shared = jnp.zeros((6 * GLL, 128), F32)
+        else:
+            shared = full_v[row - 1, pl.ds(GLL - 1, 6 * GLL, stride=GLL), :]
+        full_v[row, pl.ds(0, 6 * GLL, stride=GLL), :] = shared
+    for j in range(ROWS):
+        next_o[j] = full_v[slots[j]].reshape(3, 2, NODES, 128)
     arrived(5)
     for j in range(ROWS):
-        block = next_r[slots[j]].astype(F32)
-        for i in range(6):
-            next_o[j, i // 2, i % 2] = unpack(block, i)
-    arrived(6)
-    for j in range(ROWS):
-        start_o[j] = start_r[slots[j]].astype(F32).reshape(3, 2, NODES, 128)
-    sent(6)
+        start_o[j] = start_r[flip(slots[j])].astype(F32).reshape(3, 2, NODES, 128)
+    sent(5)
 
 
 def store_kernel(next_v, start_v, next_ref, start_ref, sem):
@@ -592,6 +678,7 @@
             vm((2, 6 * NODES, modes), LOW), vm((2, 6 * NODES, half), F32),
             vm((2, 3 * NODES, half), LOW),
             vm((2, 4, 6 * GLL * groups, 128), LOW), vm((2, 4, 6 * GLL * groups, 128), LOW),
+            vm((ROWS, 256, 128), F32), vm((ROWS,) + block, F32),
             vm((2, GLL, 128), F32), vm((2, GLL, 128), F32),
             sem((9 + ROWS,)), sem((7, ROWS)), sem((7, ROWS)), sem((2, 4)), sem((2, 4)),
             sem((2,)), sem((2,)),

time: 49.1 us -> 45.2 us (0.921)
  the two profiles are of different devices: /device:TPU:16 before, /device:TPU:8 now
where the time goes in v4:
time: 45.2 us; the launch traced here: 45 us
  Pallas kernels  44.4 us (98%)
  between operations  0.64 us (1%)
    pallas_call x1, Pallas kernels, on_device(): pl.pallas_call(run, out_shape=(held_out, held_out), in_specs=[any_spec] *...  43.2 us
    pallas_call x1, Pallas kernels, on_device(): pl.pallas_call(store_kernel, out_shape=(jax.ShapeDtypeStruct(local, F32),...  1.2 us

profile of v4, /device:TPU:8, one launch (start us, length us, event | category | flops | bytes accessed | tf_op | source)
XLA Modules:
  0.0 45.0 jit_solution(4783704698031283973)
XLA Ops:
  0.6 43.2 %shard_map.113 = (f32[4,3,2,64,128]{4,3,2,1,0:T(8,128)S(1)}, f32[4,3,2,64,128]{4,3,2,1,0:T(8,128)S(1)}) custom-call(f32[4,3,2,64,128]{4,3,2,1,0:T(8,128)} %args_0_.4, f32[4,3,2,64,128]{4,3,2,1,0:T(8,128)} %args_1_.4, bf16[4,3,2,64,128]{4,3,2,1,0:T(8,128)(2,1)} %args_2_.4, f32[2,4]{1,0:T(2,128)} %bitcast.1, s32[1,4]{1,0:T(1,128)} %args_4_.4, ...), custom_call_target="tpu_custom_call" | custom-call | flops 1900000000 | bytes 7000000 | tf_op jit(solution)/shard_map/pallas_call | solution.py:663
  43.8 1.2 %shard_map.114 = (f32[4,3,2,64,128]{4,3,2,1,0:T(8,128)}, f32[4,3,2,64,128]{4,3,2,1,0:T(8,128)}) custom-call(f32[4,3,2,64,128]{4,3,2,1,0:T(8,128)S(1)} %get-tuple-element.4.next_v, f32[4,3,2,64,128]{4,3,2,1,0:T(8,128)S(1)} %get-tuple-element.5.start_v), custom_call_target="tpu_custom_call" | custom-call | tf_op jit(solution)/shard_map/pallas_call | solution.py:698

commit v5 on v4

--- a/solution.py
+++ b/solution.py
@@ -164,17 +164,20 @@
             place = jnp.where(slots[j] == row, j, place)
         return place
 
-    whole = (0, 6 * NODES)
+    part = NODES // 2
+    halves = ((0, 6 * part), (6 * part, 12 * part))
     inner = NODES - 2 * GLL
     edges = 12 * GLL
     spare = 4
     kept = 6 * inner - spare * GLL
     phases = (
-        (0,) + whole,
+        (0,) + halves[0],
         (1, 0, edges + inner), (1, edges + inner, 6 * NODES),
         (2, 0, kept), (2, kept, kept + 6 * GLL),
-        (3,) + whole,
+        (3,) + halves[0],
         (2, kept + 6 * GLL, kept + 12 * GLL),
+        (0,) + halves[1],
+        (3,) + halves[1],
     )
 
     def unpack(block, i):
@@ -210,7 +213,11 @@
     for load in loads[2 : 2 + ROWS]:
         load.wait()
     for device in range(ROWS):
-        send_v[0, device] = flat(state_v[elem_of(flip(device))]).astype(LOW)
+        block = flat(state_v[elem_of(flip(device))]).astype(LOW)
+        for h in range(2):
+            for i in range(6):
+                begin = i * NODES + h * part
+                send_v[0, device, rows_of(6 * h + i, part), :] = block[begin : begin + part]
 
     @pl.when(early)
     def _():
@@ -229,6 +236,7 @@
         greet(0)
 
     start(0)
+    start(7)
     state_r[member] = send_v[0, member]
 
     w2_load.wait()
@@ -332,9 +340,6 @@
                 pl.ds(base + GLL, inner), :
             ].astype(LOW)
     forcing_r[member] = send_v[1, member]
-    sent(0)
-    start(1)
-
     fwd_load.wait()
     bwd_load.wait()
     lane = lax.broadcasted_iota(jnp.int32, (NODES, 3 * NODES), 1)
@@ -350,10 +355,9 @@
     )
     bwd_mat = (bwd_v[0] * coef - bwd_v[1] * (viscosity / ratio)).astype(LOW)
 
-    arrived(0)
-
-    def gathered(phase, i):
-        return jnp.concatenate([recv[phase][q, rows_of(i), :] for q in range(groups)], axis=1)
+    def state_part(h, i):
+        rows = rows_of(6 * h + i, part)
+        return jnp.concatenate([state_r[q, rows, :] for q in range(groups)], axis=1)
 
     def wide(block):
         return jnp.concatenate([block] * groups, axis=1)
@@ -369,29 +373,42 @@
     wave = mode_ids.astype(F32) * (wave_scale / modes)
 
     synth_load.wait()
-    even_v[...] = jnp.dot(
-        jnp.concatenate([gathered(0, 2 * c) for c in range(3)], axis=0),
-        synth_v[0],
-        preferred_element_type=F32,
-    )
-    odd_v[...] = jnp.dot(
-        jnp.concatenate([gathered(0, 2 * c + 1) for c in range(3)], axis=0),
-        synth_v[1],
-        preferred_element_type=F32,
-    )
-
-    for q, (left, right) in enumerate(pair_order):
-        el, ol = even_v[rows_of(left), :], odd_v[rows_of(left), :]
-        er, orr = even_v[rows_of(right), :], odd_v[rows_of(right), :]
-        prod_v[0, rows_of(q), :] = (el * er + ol * orr).astype(LOW)
-        prod_v[1, rows_of(q), :] = (el * orr + ol * er).astype(LOW)
     anal_load.wait()
-    for p in range(2):
-        modal_v[p] = jnp.dot(prod_v[p], anal_v[p], preferred_element_type=F32).astype(LOW)
+
+    def half_rows(index, h):
+        return pl.ds(index * NODES + h * part, part)
+
+    for h in range(2):
+        if h == 0:
+            arrived(0)
+        else:
+            sent(0)
+            sent(7)
+            start(1)
+            arrived(7)
+        for p, planes in ((0, even_v), (1, odd_v)):
+            values = jnp.dot(
+                jnp.concatenate([state_part(h, 2 * c + p) for c in range(3)], axis=0),
+                synth_v[p],
+                preferred_element_type=F32,
+            )
+            for c in range(3):
+                planes[half_rows(c, h), :] = values[c * part : (c + 1) * part]
+        for q, (left, right) in enumerate(pair_order):
+            el, ol = even_v[half_rows(left, h), :], odd_v[half_rows(left, h), :]
+            er, orr = even_v[half_rows(right, h), :], odd_v[half_rows(right, h), :]
+            prod_v[0, rows_of(6 * h + q, part), :] = (el * er + ol * orr).astype(LOW)
+            prod_v[1, rows_of(6 * h + q, part), :] = (el * orr + ol * er).astype(LOW)
+        for p in range(2):
+            values = jnp.dot(
+                prod_v[p, rows_of(h, 6 * part), :], anal_v[p], preferred_element_type=F32
+            ).astype(LOW)
+            for q in range(6):
+                modal_v[p, half_rows(q, h), :] = values[q * part : (q + 1) * part]
 
     for c in range(3):
         for p in range(2):
-            values = gathered(0, 2 * c + p)
+            values = jnp.concatenate([state_part(h, 2 * c + p) for h in range(2)], axis=0)
             stack = jnp.concatenate(
                 [
                     modal_v[p, rows_of(pair_index[0][c]), :],
@@ -518,39 +535,48 @@
             lateral.append((grads[:NODES], grads[NODES : 2 * NODES], wide(quad_v[...]) * (turn * other)))
         for q, (left, right) in enumerate(pair_order):
             cot = lateral[right][left] + lateral[left][right]
-            cot_v[p, rows_of(q), :] = (norm * cot).astype(LOW)
-
-    for p in range(2):
-        spread_v[p] = jnp.dot(cot_v[p], synth_v[p], preferred_element_type=F32)
-    for c in range(3):
-        even = jnp.zeros((NODES, even_v.shape[1]), F32)
-        odd = jnp.zeros((NODES, even_v.shape[1]), F32)
-        for d in range(3):
-            se = spread_v[0, rows_of(pair_index[c][d]), :]
-            so = spread_v[1, rows_of(pair_index[c][d]), :]
-            ed, od = even_v[rows_of(d), :], odd_v[rows_of(d), :]
-            even = even + (se * ed + so * od)
-            odd = odd + (se * od + so * ed)
-        pcot_v[0, rows_of(c), :] = even.astype(LOW)
-        pcot_v[1, rows_of(c), :] = odd.astype(LOW)
+            cot = (norm * cot).astype(LOW)
+            for h in range(2):
+                cot_v[p, rows_of(6 * h + q, part), :] = cot[h * part : (h + 1) * part]
+
     gain = jnp.where(mode_ids == 0, 3.0 * modes * time_step, 6.0 * modes * time_step).astype(F32)
-    for p in range(2):
-        back = jnp.dot(pcot_v[p], anal_v[p], preferred_element_type=F32)
+    gain = gain[:part]
+    for h in range(2):
+        for p in range(2):
+            spread_v[p] = jnp.dot(
+                cot_v[p, rows_of(h, 6 * part), :], synth_v[p], preferred_element_type=F32
+            )
         for c in range(3):
-            low = (
-                field(num_v, 2 * c + p) + gain * back[c * NODES : (c + 1) * NODES]
-            ).astype(LOW)
-            for q in range(groups):
-                send_v[3, q, rows_of(2 * c + p), :] = low[:, q * 128 : (q + 1) * 128]
+            even = jnp.zeros((part, even_v.shape[1]), F32)
+            odd = jnp.zeros((part, even_v.shape[1]), F32)
+            for d in range(3):
+                se = spread_v[0, rows_of(pair_index[c][d], part), :]
+                so = spread_v[1, rows_of(pair_index[c][d], part), :]
+                ed, od = even_v[half_rows(d, h), :], odd_v[half_rows(d, h), :]
+                even = even + (se * ed + so * od)
+                odd = odd + (se * od + so * ed)
+            pcot_v[0, rows_of(c, part), :] = even.astype(LOW)
+            pcot_v[1, rows_of(c, part), :] = odd.astype(LOW)
+        for p in range(2):
+            back = jnp.dot(pcot_v[p], anal_v[p], preferred_element_type=F32)
+            for c in range(3):
+                i = 2 * c + p
+                near = gain * back[c * part : (c + 1) * part]
+                for q in range(groups):
+                    rest = num_v[half_rows(6 * q + i, h), :]
+                    send_v[3, q, rows_of(6 * h + i, part), :] = (
+                        rest + near[:, q * 128 : (q + 1) * 128]
+                    ).astype(LOW)
+        if h == 0:
+            sent(3)
+            sent(4)
+
+            @pl.when(across_high)
+            def _():
+                sent(6)
+
+        start((5, 8)[h])
     start_r[member] = send_v[3, member]
-    sent(3)
-    sent(4)
-
-    @pl.when(across_high)
-    def _():
-        sent(6)
-
-    start(5)
 
     around_sent(0)
     around_sent(1)
@@ -621,9 +647,15 @@
     for j in range(ROWS):
         next_o[j] = full_v[slots[j]].reshape(3, 2, NODES, 128)
     arrived(5)
+    arrived(8)
     for j in range(ROWS):
-        start_o[j] = start_r[flip(slots[j])].astype(F32).reshape(3, 2, NODES, 128)
+        block = start_r[flip(slots[j])].astype(F32)
+        for h in range(2):
+            for i in range(6):
+                begin = (6 * h + i) * part
+                start_o[j, i // 2, i % 2, rows_of(h, part), :] = block[begin : begin + part]
     sent(5)
+    sent(8)
 
 
 def store_kernel(next_v, start_v, next_ref, start_ref, sem):
@@ -675,12 +707,12 @@
             vm((3 * NODES, half), F32), vm((3 * NODES, half), F32),
             vm((2, 6 * NODES, half), LOW), vm((2, 6 * NODES, modes), LOW),
             vm((6 * NODES * groups, 128), F32), vm((6 * NODES * groups, 128), F32),
-            vm((2, 6 * NODES, modes), LOW), vm((2, 6 * NODES, half), F32),
-            vm((2, 3 * NODES, half), LOW),
+            vm((2, 6 * NODES, modes), LOW), vm((2, 3 * NODES, half), F32),
+            vm((2, 3 * NODES // 2, half), LOW),
             vm((2, 4, 6 * GLL * groups, 128), LOW), vm((2, 4, 6 * GLL * groups, 128), LOW),
             vm((ROWS, 256, 128), F32), vm((ROWS,) + block, F32),
             vm((2, GLL, 128), F32), vm((2, GLL, 128), F32),
-            sem((9 + ROWS,)), sem((7, ROWS)), sem((7, ROWS)), sem((2, 4)), sem((2, 4)),
+            sem((9 + ROWS,)), sem((9, ROWS)), sem((9, ROWS)), sem((2, 4)), sem((2, 4)),
             sem((2,)), sem((2,)),
         ],
         compiler_params=pltpu.CompilerParams(

time: 45.2 us -> 44.4 us (0.982)
  the two profiles are of different devices: /device:TPU:8 before, /device:TPU:16 now
where the time goes in v5:
time: 44.4 us; the launch traced here: 44.3 us
  Pallas kernels  43.7 us (98%)
  between operations  0.64 us (1%)
    pallas_call x1, Pallas kernels, on_device(): pl.pallas_call(run, out_shape=(held_out, held_out), in_specs=[any_spec] *...  42.5 us
    pallas_call x1, Pallas kernels, on_device(): pl.pallas_call(store_kernel, out_shape=(jax.ShapeDtypeStruct(local, F32),...  1.2 us

profile of v5, /device:TPU:16, one launch (start us, length us, event | category | flops | bytes accessed | tf_op | source)
XLA Modules:
  0.0 44.3 jit_solution(11334670435783397251)
XLA Ops:
  0.6 42.5 %shard_map.113 = (f32[4,3,2,64,128]{4,3,2,1,0:T(8,128)S(1)}, f32[4,3,2,64,128]{4,3,2,1,0:T(8,128)S(1)}) custom-call(f32[4,3,2,64,128]{4,3,2,1,0:T(8,128)} %args_0_.4, f32[4,3,2,64,128]{4,3,2,1,0:T(8,128)} %args_1_.4, bf16[4,3,2,64,128]{4,3,2,1,0:T(8,128)(2,1)} %args_2_.4, f32[2,4]{1,0:T(2,128)} %bitcast.1, s32[1,4]{1,0:T(1,128)} %args_4_.4, ...), custom_call_target="tpu_custom_call" | custom-call | flops 1900000000 | bytes 7000000 | tf_op jit(solution)/shard_map/pallas_call | solution.py:695
  43.1 1.2 %shard_map.114 = (f32[4,3,2,64,128]{4,3,2,1,0:T(8,128)}, f32[4,3,2,64,128]{4,3,2,1,0:T(8,128)}) custom-call(f32[4,3,2,64,128]{4,3,2,1,0:T(8,128)S(1)} %get-tuple-element.4.next_v, f32[4,3,2,64,128]{4,3,2,1,0:T(8,128)S(1)} %get-tuple-element.5.start_v), custom_call_target="tpu_custom_call" | custom-call | tf_op jit(solution)/shard_map/pallas_call | solution.py:730

commit v6 on v5

--- a/solution.py
+++ b/solution.py
@@ -167,23 +167,20 @@
     part = NODES // 2
     halves = ((0, 6 * part), (6 * part, 12 * part))
     inner = NODES - 2 * GLL
-    edges = 12 * GLL
+    edges = 6 * GLL
+    far = edges + 6 * inner
     spare = 4
     kept = 6 * inner - spare * GLL
     phases = (
         (0,) + halves[0],
-        (1, 0, edges + inner), (1, edges + inner, 6 * NODES),
+        (1, 0, edges), (1, edges, far),
         (2, 0, kept), (2, kept, kept + 6 * GLL),
         (3,) + halves[0],
         (2, kept + 6 * GLL, kept + 12 * GLL),
         (0,) + halves[1],
         (3,) + halves[1],
-    )
-
-    def unpack(block, i):
-        sides = block[i * 2 * GLL : (i + 1) * 2 * GLL]
-        middle = block[edges + i * inner : edges + (i + 1) * inner]
-        return jnp.concatenate([sides[:GLL], middle, sides[GLL:]], axis=0)
+        (1, far, 6 * NODES),
+    )
 
     def swap(phase, partner, arrival=False):
         which, begin, end = phases[phase]
@@ -329,16 +326,44 @@
         both = psi_v[lower, :] + psi_v[upper, :]
         psi_v[lower, :] = both
         psi_v[upper, :] = both
+    slab_edge = pltpu.make_async_remote_copy(
+        src_ref=edge_send.at[0, 1],
+        dst_ref=edge_recv.at[0, 1],
+        send_sem=esend_sem.at[0, 1],
+        recv_sem=erecv_sem.at[0, 1],
+        device_id={"elems": high_slab},
+        device_id_type=MESH,
+    )
+    edge_send[0, 1] = jnp.concatenate(
+        [psi_v[pl.ds((i + 1) * NODES - GLL, GLL), :] for i in range(6 * ROWS)], axis=0
+    ).astype(LOW)
+
+    @pl.when(jnp.logical_not(across_high))
+    def _():
+        slab_edge.start()
+
     for row in range(ROWS):
         device = flip(row)
         for i in range(6):
             base = (6 * row + i) * NODES
-            send_v[1, device, pl.ds(i * 2 * GLL, 2 * GLL), :] = jnp.concatenate(
-                [psi_v[pl.ds(base, GLL), :], psi_v[pl.ds(base + NODES - GLL, GLL), :]], axis=0
-            ).astype(LOW)
             send_v[1, device, pl.ds(edges + i * inner, inner), :] = psi_v[
                 pl.ds(base + GLL, inner), :
             ].astype(LOW)
+
+    @pl.when(jnp.logical_not(across_low))
+    def _():
+        slab_edge.wait_recv()
+        came = edge_recv[0, 1].astype(F32)
+        for i in range(6 * ROWS):
+            rows = pl.ds(i * NODES, GLL)
+            psi_v[rows, :] = psi_v[rows, :] + came[i * GLL : (i + 1) * GLL]
+
+    for row in range(ROWS):
+        device = flip(row)
+        for begin, offset in ((0, 0), (far, NODES - GLL)):
+            send_v[1, device, pl.ds(begin, edges), :] = jnp.concatenate(
+                [psi_v[pl.ds((6 * row + i) * NODES + offset, GLL), :] for i in range(6)], axis=0
+            ).astype(LOW)
     forcing_r[member] = send_v[1, member]
     fwd_load.wait()
     bwd_load.wait()
@@ -385,6 +410,11 @@
             sent(0)
             sent(7)
             start(1)
+
+            @pl.when(across_high)
+            def _():
+                start(9)
+
             arrived(7)
         for p, planes in ((0, even_v), (1, odd_v)):
             values = jnp.dot(
@@ -447,13 +477,19 @@
     mass_copy(1).start()
     arrived(1)
     for q in range(groups):
-        block = forcing_r[q, pl.ds(0, edges), :].astype(F32)
-        for way, begin in ((2, GLL), (3, 0)):
-            edge_send[0, way, pl.ds(q * 6 * GLL, 6 * GLL), :] = jnp.concatenate(
-                [block[i * 2 * GLL + begin : i * 2 * GLL + begin + GLL] for i in range(6)], axis=0
-            ).astype(LOW)
-    edge_copy(0, 2).start()
+        edge_send[0, 3, pl.ds(q * edges, edges), :] = forcing_r[q, pl.ds(0, edges), :]
     edge_copy(0, 3).start()
+
+    @pl.when(across_high)
+    def _():
+        arrived(9)
+        for q in range(groups):
+            edge_send[0, 2, pl.ds(q * edges, edges), :] = forcing_r[q, pl.ds(far, edges), :]
+        edge_copy(0, 2).start()
+
+    @pl.when(jnp.logical_not(across_high))
+    def _():
+        edge_send[0, 2] = jnp.zeros((edge_rows, 128), LOW)
 
     @pl.when(row_here > 0)
     def _():
@@ -482,8 +518,6 @@
                     stage_v[q, pl.ds(k * GLL * GLL, GLL, stride=GLL), :] = tile
         send_v[2, q, pl.ds(0, kept), :] = stage_v[q].astype(LOW)
     next_r[member, pl.ds(0, kept), :] = send_v[2, member, pl.ds(0, kept), :]
-    sent(1)
-    sent(2)
     start(3)
     mass_copy(0).wait()
     mass_copy(1).wait()
@@ -509,11 +543,24 @@
 
     arrived(2)
     for q in range(groups):
-        block = forcing_r[q].astype(F32)
+        block = forcing_r[q, pl.ds(0, far), :].astype(F32)
         for i in range(6):
-            rows = rows_of(6 * q + i)
-            psi_v[rows, :] = unpack(block, i)
-    add_around(0, psi_v)
+            base = (6 * q + i) * NODES
+            psi_v[pl.ds(base, GLL), :] = block[i * GLL : (i + 1) * GLL]
+            psi_v[pl.ds(base + GLL, inner), :] = block[edges + i * inner : edges + (i + 1) * inner]
+    edge_copy(0, 3).wait_recv()
+    far_edge = edge_send[0, 2].astype(F32) + edge_recv[0, 3].astype(F32)
+    for i in range(6 * groups):
+        psi_v[pl.ds((i + 1) * NODES - GLL, GLL), :] = far_edge[i * GLL : (i + 1) * GLL]
+
+    @pl.when(across_low)
+    def _():
+        edge_copy(0, 2).wait_recv()
+        came = edge_recv[0, 2].astype(F32)
+        for i in range(6 * groups):
+            rows = pl.ds(i * NODES, GLL)
+            psi_v[rows, :] = psi_v[rows, :] + came[i * GLL : (i + 1) * GLL]
+
     for i in range(6 * groups):
         rows = rows_of(i)
         psi_v[rows, :] = scale_v[...] * (psi_v[rows, :] + mult_v[...] * num_v[rows, :])
@@ -567,19 +614,30 @@
                     send_v[3, q, rows_of(6 * h + i, part), :] = (
                         rest + near[:, q * 128 : (q + 1) * 128]
                     ).astype(LOW)
-        if h == 0:
-            sent(3)
-            sent(4)
-
-            @pl.when(across_high)
-            def _():
-                sent(6)
-
         start((5, 8)[h])
     start_r[member] = send_v[3, member]
 
-    around_sent(0)
+    sent(1)
+    sent(2)
+    sent(3)
+    sent(4)
+
+    @pl.when(across_high)
+    def _():
+        sent(6)
+
+    edge_copy(0, 3).wait_send()
     around_sent(1)
+
+    @pl.when(across_high)
+    def _():
+        sent(9)
+        edge_copy(0, 2).wait_send()
+
+    @pl.when(jnp.logical_not(across_high))
+    def _():
+        slab_edge.wait_send()
+
 
     @pl.when(row_here < ROWS - 1)
     def _():
@@ -712,7 +770,7 @@
             vm((2, 4, 6 * GLL * groups, 128), LOW), vm((2, 4, 6 * GLL * groups, 128), LOW),
             vm((ROWS, 256, 128), F32), vm((ROWS,) + block, F32),
             vm((2, GLL, 128), F32), vm((2, GLL, 128), F32),
-            sem((9 + ROWS,)), sem((9, ROWS)), sem((9, ROWS)), sem((2, 4)), sem((2, 4)),
+            sem((9 + ROWS,)), sem((10, ROWS)), sem((10, ROWS)), sem((2, 4)), sem((2, 4)),
             sem((2,)), sem((2,)),
         ],
         compiler_params=pltpu.CompilerParams(

time: 44.4 us -> 43.6 us (0.982)
  the two profiles are of different devices: /device:TPU:16 before, /device:TPU:8 now
where the time goes in v6:
time: 43.6 us; the launch traced here: 43.4 us
  Pallas kernels  42.8 us (98%)
  between operations  0.64 us (1%)
    pallas_call x1, Pallas kernels, on_device(): pl.pallas_call(run, out_shape=(held_out, held_out), in_specs=[any_spec] *...  41.6 us
    pallas_call x1, Pallas kernels, on_device(): pl.pallas_call(store_kernel, out_shape=(jax.ShapeDtypeStruct(local, F32),...  1.2 us

profile of v6, /device:TPU:8, one launch (start us, length us, event | category | flops | bytes accessed | tf_op | source)
XLA Modules:
  0.0 43.4 jit_solution(5381134061145245008)
XLA Ops:
  0.6 41.6 %shard_map.113 = (f32[4,3,2,64,128]{4,3,2,1,0:T(8,128)S(1)}, f32[4,3,2,64,128]{4,3,2,1,0:T(8,128)S(1)}) custom-call(f32[4,3,2,64,128]{4,3,2,1,0:T(8,128)} %args_0_.4, f32[4,3,2,64,128]{4,3,2,1,0:T(8,128)} %args_1_.4, bf16[4,3,2,64,128]{4,3,2,1,0:T(8,128)(2,1)} %args_2_.4, f32[2,4]{1,0:T(2,128)} %bitcast.1, s32[1,4]{1,0:T(1,128)} %args_4_.4, ...), custom_call_target="tpu_custom_call" | custom-call | flops 1900000000 | bytes 7000000 | tf_op jit(solution)/shard_map/pallas_call | solution.py:753
  42.2 1.2 %shard_map.114 = (f32[4,3,2,64,128]{4,3,2,1,0:T(8,128)}, f32[4,3,2,64,128]{4,3,2,1,0:T(8,128)}) custom-call(f32[4,3,2,64,128]{4,3,2,1,0:T(8,128)S(1)} %get-tuple-element.4.next_v, f32[4,3,2,64,128]{4,3,2,1,0:T(8,128)S(1)} %get-tuple-element.5.start_v), custom_call_target="tpu_custom_call" | custom-call | tf_op jit(solution)/shard_map/pallas_call | solution.py:788

commit v7 on v6

--- a/solution.py
+++ b/solution.py
@@ -82,7 +82,7 @@
     state_ref, adj_ref, obs_ref, spacing_h, slot_h, synth_ref, anal_ref, fwd_ref, bwd_ref, w2_ref,
     next_o, start_o,
     spacing_ref, slot_ref, state_v, adj_v, obs_v, synth_v, anal_v, fwd_v, bwd_v, w2_v,
-    send_v, state_r, forcing_r, next_r, start_r, quad_v, scale_v, mult_v,
+    send_v, state_r, forcing_r, next_r, start_a, start_b, quad_v, scale_v, mult_v,
     even_v, odd_v, prod_v, modal_v, num_v, psi_v, cot_v, spread_v, pcot_v,
     edge_send, edge_recv, stage_v, full_v, mass_send, mass_recv,
     load_sem, send_sem, recv_sem, esend_sem, erecv_sem, msend_sem, mrecv_sem,
@@ -93,7 +93,7 @@
     high_slab = lax.rem(slab + 1, slabs)
     partners = (lax.rem(member + 2, 4), 3 - member, member + 1 - 2 * lax.rem(member, 2))
     modes = groups * 128
-    recv = (state_r, forcing_r, next_r, start_r)
+    recv = (state_r, forcing_r, next_r, start_a)
 
     loads = [
         pltpu.make_async_copy(src, dst, load_sem.at[i])
@@ -186,9 +186,15 @@
         which, begin, end = phases[phase]
         rows = pl.ds(begin, end - begin)
         slot = partner if arrival else member
+        if phase == 8:
+            target = start_b.at[slot]
+        elif phase == 5:
+            target = start_a.at[slot]
+        else:
+            target = recv[which].at[slot, rows]
         return pltpu.make_async_remote_copy(
             src_ref=send_v.at[which, partner, rows],
-            dst_ref=recv[which].at[slot, rows],
+            dst_ref=target,
             send_sem=send_sem.at[phase, partner],
             recv_sem=recv_sem.at[phase, slot],
             device_id={"modes": partner},
@@ -615,7 +621,8 @@
                         rest + near[:, q * 128 : (q + 1) * 128]
                     ).astype(LOW)
         start((5, 8)[h])
-    start_r[member] = send_v[3, member]
+    start_a[member] = send_v[3, member, rows_of(0, 6 * part), :]
+    start_b[member] = send_v[3, member, rows_of(1, 6 * part), :]
 
     sent(1)
     sent(2)
@@ -704,23 +711,20 @@
         full_v[row, pl.ds(0, 6 * GLL, stride=GLL), :] = shared
     for j in range(ROWS):
         next_o[j] = full_v[slots[j]].reshape(3, 2, NODES, 128)
-    arrived(5)
-    arrived(8)
-    for j in range(ROWS):
-        block = start_r[flip(slots[j])].astype(F32)
-        for h in range(2):
+    for h, (phase, rows) in enumerate(((5, start_a), (8, start_b))):
+        arrived(phase)
+        for j in range(ROWS):
+            block = rows[flip(slots[j])].astype(F32)
             for i in range(6):
-                begin = (6 * h + i) * part
-                start_o[j, i // 2, i % 2, rows_of(h, part), :] = block[begin : begin + part]
+                start_o[j, i // 2, i % 2, rows_of(h, part), :] = block[i * part : (i + 1) * part]
     sent(5)
     sent(8)
 
 
 def store_kernel(next_v, start_v, next_ref, start_ref, sem):
     stores = [
-        pltpu.make_async_copy(source.at[j], target.at[j], sem.at[which, j])
+        pltpu.make_async_copy(source, target, sem.at[which])
         for which, (source, target) in enumerate(((next_v, next_ref), (start_v, start_ref)))
-        for j in range(ROWS)
     ]
     for store in stores:
         store.start()
@@ -760,7 +764,8 @@
             vm(local, F32), vm(local, F32), vm(local, LOW),
             vm((2, modes, half), LOW), vm((2, half, modes), LOW),
             vm((2, NODES, 3 * NODES), F32), vm((2, 3 * NODES, NODES), F32), vm((NODES, 128), F32),
-            vm((4, ROWS) + block, LOW), *[vm((ROWS,) + block, LOW)] * 4,
+            vm((4, ROWS) + block, LOW), *[vm((ROWS,) + block, LOW)] * 3,
+            *[vm((ROWS, 3 * NODES, 128), LOW)] * 2,
             vm((NODES, 128), F32), vm((NODES, 128), F32), vm((NODES, 128), F32),
             vm((3 * NODES, half), F32), vm((3 * NODES, half), F32),
             vm((2, 6 * NODES, half), LOW), vm((2, 6 * NODES, modes), LOW),
@@ -790,7 +795,7 @@
         out_shape=(jax.ShapeDtypeStruct(local, F32), jax.ShapeDtypeStruct(local, F32)),
         in_specs=[pl.BlockSpec(memory_space=pl.ANY)] * 2,
         out_specs=(any_spec, any_spec),
-        scratch_shapes=[sem((2, ROWS))],
+        scratch_shapes=[sem((2,))],
         compiler_params=pltpu.CompilerParams(vmem_limit_bytes=1024 * 1024),
     )(next_v, start_v)
 

time: 43.6 us -> 43.5 us (level)
  no operation moved by 1% of the time
where the time goes in v7:
time: 43.5 us; the launch traced here: 43.4 us
  Pallas kernels  42.7 us (98%)
  between operations  0.64 us (1%)
    pallas_call x1, Pallas kernels, on_device(): pl.pallas_call(run, out_shape=(held_out, held_out), in_specs=[any_spec] *...  41.6 us
    pallas_call x1, Pallas kernels, on_device(): pl.pallas_call(store_kernel, out_shape=(jax.ShapeDtypeStruct(local, F32),...  1.16 us

profile of v7, /device:TPU:8, one launch (start us, length us, event | category | flops | bytes accessed | tf_op | source)
XLA Modules:
  0.0 43.4 jit_solution(16724471009527382835)
XLA Ops:
  0.6 41.6 %shard_map.113 = (f32[4,3,2,64,128]{4,3,2,1,0:T(8,128)S(1)}, f32[4,3,2,64,128]{4,3,2,1,0:T(8,128)S(1)}) custom-call(f32[4,3,2,64,128]{4,3,2,1,0:T(8,128)} %args_0_.4, f32[4,3,2,64,128]{4,3,2,1,0:T(8,128)} %args_1_.4, bf16[4,3,2,64,128]{4,3,2,1,0:T(8,128)(2,1)} %args_2_.4, f32[2,4]{1,0:T(2,128)} %bitcast.1, s32[1,4]{1,0:T(1,128)} %args_4_.4, ...), custom_call_target="tpu_custom_call" | custom-call | flops 1900000000 | bytes 7000000 | tf_op jit(solution)/shard_map/pallas_call | solution.py:757
  42.2 1.2 %shard_map.114 = (f32[4,3,2,64,128]{4,3,2,1,0:T(8,128)}, f32[4,3,2,64,128]{4,3,2,1,0:T(8,128)}) custom-call(f32[4,3,2,64,128]{4,3,2,1,0:T(8,128)S(1)} %get-tuple-element.4.next_v, f32[4,3,2,64,128]{4,3,2,1,0:T(8,128)S(1)} %get-tuple-element.5.start_v), custom_call_target="tpu_custom_call" | custom-call | tf_op jit(solution)/shard_map/pallas_call | solution.py:793

commit v8 on v6

--- a/solution.py
+++ b/solution.py
@@ -519,6 +519,15 @@
         send_v[2, q, pl.ds(0, kept), :] = stage_v[q].astype(LOW)
     next_r[member, pl.ds(0, kept), :] = send_v[2, member, pl.ds(0, kept), :]
     start(3)
+    arrived(2)
+    for q in range(groups):
+        block = forcing_r[q, pl.ds(edges, 6 * inner), :].astype(F32)
+        for i in range(6):
+            rows = pl.ds((6 * q + i) * NODES + GLL, inner)
+            inside = pl.ds(GLL, inner)
+            psi_v[rows, :] = scale_v[inside, :] * (
+                block[i * inner : (i + 1) * inner] + mult_v[inside, :] * num_v[rows, :]
+            )
     mass_copy(0).wait()
     mass_copy(1).wait()
     scale_v[:GLL, :] = keep[:GLL] / (mass_send[1] + mass_recv[0])
@@ -541,17 +550,16 @@
     def _():
         start(6)
 
-    arrived(2)
+    edge_copy(0, 3).wait_recv()
+    far_edge = edge_send[0, 2].astype(F32) + edge_recv[0, 3].astype(F32)
     for q in range(groups):
-        block = forcing_r[q, pl.ds(0, far), :].astype(F32)
+        near_edge = forcing_r[q, pl.ds(0, edges), :].astype(F32)
         for i in range(6):
             base = (6 * q + i) * NODES
-            psi_v[pl.ds(base, GLL), :] = block[i * GLL : (i + 1) * GLL]
-            psi_v[pl.ds(base + GLL, inner), :] = block[edges + i * inner : edges + (i + 1) * inner]
-    edge_copy(0, 3).wait_recv()
-    far_edge = edge_send[0, 2].astype(F32) + edge_recv[0, 3].astype(F32)
-    for i in range(6 * groups):
-        psi_v[pl.ds((i + 1) * NODES - GLL, GLL), :] = far_edge[i * GLL : (i + 1) * GLL]
+            psi_v[pl.ds(base, GLL), :] = near_edge[i * GLL : (i + 1) * GLL]
+            psi_v[pl.ds(base + NODES - GLL, GLL), :] = far_edge[
+                (6 * q + i) * GLL : (6 * q + i + 1) * GLL
+            ]
 
     @pl.when(across_low)
     def _():
@@ -562,8 +570,10 @@
             psi_v[rows, :] = psi_v[rows, :] + came[i * GLL : (i + 1) * GLL]
 
     for i in range(6 * groups):
-        rows = rows_of(i)
-        psi_v[rows, :] = scale_v[...] * (psi_v[rows, :] + mult_v[...] * num_v[rows, :])
+        for begin in (0, NODES - GLL):
+            side = pl.ds(begin, GLL)
+            rows = pl.ds(i * NODES + begin, GLL)
+            psi_v[rows, :] = scale_v[side, :] * (psi_v[rows, :] + mult_v[side, :] * num_v[rows, :])
 
     norm = jnp.where(mode_ids == 0, 1.0 / (3.0 * modes), 0.5 / (3.0 * modes)).astype(F32)
     for p in range(2):

time: 43.6 us -> 43.5 us (level)
  no operation moved by 1% of the time
where the time goes in v8:
time: 43.5 us; the launch traced here: 43.4 us
  Pallas kernels  42.8 us (98%)
  between operations  0.64 us (1%)
    pallas_call x1, Pallas kernels, on_device(): pl.pallas_call(run, out_shape=(held_out, held_out), in_specs=[any_spec] *...  41.6 us
    pallas_call x1, Pallas kernels, on_device(): pl.pallas_call(store_kernel, out_shape=(jax.ShapeDtypeStruct(local, F32),...  1.2 us

profile of v8, /device:TPU:8, one launch (start us, length us, event | category | flops | bytes accessed | tf_op | source)
XLA Modules:
  0.0 43.4 jit_solution(10632483385944437912)
XLA Ops:
  0.6 41.6 %shard_map.113 = (f32[4,3,2,64,128]{4,3,2,1,0:T(8,128)S(1)}, f32[4,3,2,64,128]{4,3,2,1,0:T(8,128)S(1)}) custom-call(f32[4,3,2,64,128]{4,3,2,1,0:T(8,128)} %args_0_.4, f32[4,3,2,64,128]{4,3,2,1,0:T(8,128)} %args_1_.4, bf16[4,3,2,64,128]{4,3,2,1,0:T(8,128)(2,1)} %args_2_.4, f32[2,4]{1,0:T(2,128)} %bitcast.1, s32[1,4]{1,0:T(1,128)} %args_4_.4, ...), custom_call_target="tpu_custom_call" | custom-call | flops 1900000000 | bytes 7000000 | tf_op jit(solution)/shard_map/pallas_call | solution.py:763
  42.2 1.2 %shard_map.114 = (f32[4,3,2,64,128]{4,3,2,1,0:T(8,128)}, f32[4,3,2,64,128]{4,3,2,1,0:T(8,128)}) custom-call(f32[4,3,2,64,128]{4,3,2,1,0:T(8,128)S(1)} %get-tuple-element.4.next_v, f32[4,3,2,64,128]{4,3,2,1,0:T(8,128)S(1)} %get-tuple-element.5.start_v), custom_call_target="tpu_custom_call" | custom-call | tf_op jit(solution)/shard_map/pallas_call | solution.py:798
